TPU v7x, 128 devices: a whole 4x4x4 slice. The times are simulated.
128 devices in a mesh: group: 4 (over y), ingroup: 32 (over x, z, core).
Axes of the slice: x: 4, y: 4, z: 4, core: 2. Of those that a mesh axis runs over, the one named last changes fastest.
Arguments:
- tokens: bfloat16 [16384, 2048], P(('group', 'ingroup')), may hold values from -6 to 6
- cotangent: bfloat16 [16384, 2048], P(('group', 'ingroup')), may hold values from -6 to 6
- routes: int32 [16384, 8], P(('group', 'ingroup')), may hold values from 0 to 127, all different within a row; in each aligned block of 128 rows (0 to 127, 128 to 255, ...) at most 10 rows name the same one
- gate_weights: float32 [16384, 8], P(('group', 'ingroup')), may hold values from 0.1 to 1
- weight_gate: bfloat16 [128, 2048, 768], P(('group', 'ingroup')), may hold values from -0.125 to 0.125
- weight_up: bfloat16 [128, 2048, 768], P(('group', 'ingroup')), may hold values from -0.125 to 0.125
- weight_down: bfloat16 [128, 768, 2048], P(('group', 'ingroup')), may hold values from -0.21875 to 0.21875
Outputs:
- mixed: bfloat16 [16384, 2048], P(('group', 'ingroup'))
- grad_tokens: bfloat16 [16384, 2048], P(('group', 'ingroup'))
- grad_gates: float32 [16384, 8], P(('group', 'ingroup'))
- grad_weight_gate: bfloat16 [128, 2048, 768], P(('group', 'ingroup'))
- grad_weight_up: bfloat16 [128, 2048, 768], P(('group', 'ingroup'))
- grad_weight_down: bfloat16 [128, 768, 2048], P(('group', 'ingroup'))
Inputs may be any that keep to these rules, and one draw needn't show every extreme that they name: `routes`: each row names 8 different experts. Among the rows of one device no expert is named more than 10 times, and in every draw some expert is named exactly 10 times by the rows of some device.
All inputs are finite; a program needn't handle non-finite values.
Results may differ from a plain program's by a relative error of at most 0.015.
Values may be sent and summed in bfloat16 or wider, within the bound.
A program may use at most 192 MiB of HBM per device.

v0:
```python
import jax
import jax.numpy as jnp
from jax import lax
from jax.sharding import PartitionSpec as P


def expert_pass(inputs, upstream, w_gate, w_up, w_down):
    gate_pre = jnp.dot(inputs, w_gate, preferred_element_type=jnp.float32)
    up_pre = jnp.dot(inputs, w_up, preferred_element_type=jnp.float32)
    sigmoid = jax.nn.sigmoid(gate_pre)
    swish = gate_pre * sigmoid
    hidden = (swish * up_pre).astype(jnp.bfloat16)
    output = jnp.dot(hidden, w_down, preferred_element_type=jnp.float32).astype(jnp.bfloat16)
    d_hidden = jnp.dot(upstream, w_down.T, preferred_element_type=jnp.float32)
    grad_down = jnp.dot(hidden.T, upstream, preferred_element_type=jnp.float32).astype(jnp.bfloat16)
    d_gate = (d_hidden * up_pre * sigmoid * (1.0 + gate_pre * (1.0 - sigmoid))).astype(jnp.bfloat16)
    d_up = (d_hidden * swish).astype(jnp.bfloat16)
    grad_gate = jnp.dot(inputs.T, d_gate, preferred_element_type=jnp.float32).astype(jnp.bfloat16)
    grad_up = jnp.dot(inputs.T, d_up, preferred_element_type=jnp.float32).astype(jnp.bfloat16)
    d_inputs = (
        jnp.dot(d_gate, w_gate.T, preferred_element_type=jnp.float32)
        + jnp.dot(d_up, w_up.T, preferred_element_type=jnp.float32)
    ).astype(jnp.bfloat16)
    return (output, d_inputs, grad_gate, grad_up, grad_down)


def travel_one(block):
    return lax.all_to_all(block, ("group", "ingroup"), split_axis=0, concat_axis=0, tiled=True)


def body(tokens, cotangent, routes, gate_weights, weight_gate, weight_up, weight_down):
    experts_all = lax.axis_size("group") * lax.axis_size("ingroup")
    token_count, choose_count = routes.shape
    feature_count = tokens.shape[1]
    capacity = max(2, token_count * choose_count * 4 // (3 * experts_all))
    flat_routes = routes.reshape(-1)
    onehot = (flat_routes[:, None] == jnp.arange(experts_all, dtype=jnp.int32)[None, :]).astype(
        jnp.int32
    )
    position = jnp.sum((jnp.cumsum(onehot, axis=0) - onehot) * onehot, axis=1)
    slot_index = flat_routes * capacity + position
    matches = (
        slot_index.reshape(token_count, choose_count)[None, :, :]
        == jnp.arange(experts_all * capacity, dtype=jnp.int32)[:, None, None]
    )
    select = jnp.any(matches, axis=2).astype(jnp.bfloat16)
    slot_gate = jnp.sum(jnp.where(matches, gate_weights[None, :, :], 0.0), axis=(1, 2))
    outgoing = jnp.dot(select, tokens, preferred_element_type=jnp.float32).astype(jnp.bfloat16)
    outgoing = outgoing.reshape(experts_all, capacity, feature_count)
    cot_rows = jnp.dot(select, cotangent, preferred_element_type=jnp.float32)
    upstream = (
        (slot_gate[:, None] * cot_rows)
        .astype(jnp.bfloat16)
        .reshape(experts_all, capacity, feature_count)
    )
    flat_shape = (experts_all * capacity, feature_count)
    arrived = travel_one(outgoing)
    arrived_up = travel_one(upstream)
    output, d_inputs, grad_gate, grad_up, grad_down = expert_pass(
        arrived.reshape(flat_shape),
        arrived_up.reshape(flat_shape),
        weight_gate[0],
        weight_up[0],
        weight_down[0],
    )
    back_out = travel_one(output.reshape(outgoing.shape))
    back_grad = travel_one(d_inputs.reshape(outgoing.shape))
    picked = jnp.take(back_out.reshape(flat_shape), slot_index, axis=0).astype(jnp.float32)
    picked = picked.reshape(token_count, choose_count, feature_count)
    mixed = jnp.sum(gate_weights[:, :, None] * picked, axis=1).astype(jnp.bfloat16)
    grad_gates = jnp.sum(picked * cotangent.astype(jnp.float32)[:, None, :], axis=2)
    picked_grad = jnp.take(back_grad.reshape(flat_shape), slot_index, axis=0).astype(jnp.float32)
    grad_tokens = jnp.sum(
        picked_grad.reshape(token_count, choose_count, feature_count), axis=1
    ).astype(jnp.bfloat16)
    return (mixed, grad_tokens, grad_gates, grad_gate[None], grad_up[None], grad_down[None])


def solution(mesh):
    in_specs = (
        P(("group", "ingroup"), None),
        P(("group", "ingroup"), None),
        P(("group", "ingroup"), None),
        P(("group", "ingroup"), None),
        P(("group", "ingroup"), None, None),
        P(("group", "ingroup"), None, None),
        P(("group", "ingroup"), None, None),
    )
    out_specs = (
        P(("group", "ingroup"), None),
        P(("group", "ingroup"), None),
        P(("group", "ingroup"), None),
        P(("group", "ingroup"), None, None),
        P(("group", "ingroup"), None, None),
        P(("group", "ingroup"), None, None),
    )
    return jax.shard_map(body, mesh=mesh, in_specs=in_specs, out_specs=out_specs, check_vma=False)
```

profile of v0, /device:TPU:7, one launch (start us, length us, event | category | flops | bytes accessed | tf_op | source)
XLA Modules:
  0.0 542.7 jit_solution(10080959458980266417)
XLA Ops:
  14.8 9.5 %reshape.81 = bf16[128,10,2048]{2,1,0:T(8,128)(2,1)} reshape(bf16[1280,2048]{1,0:T(8,128)(2,1)} %convolution_convert_fusion.1) | data formatting | bytes 10485760 | tf_op jit(solution)/shard_map/reshape | solution.py:49
  24.4 11.2 %all-to-all-start = ((bf16[128,10,2048]{2,1,0:T(8,128)(2,1)}), bf16[128,10,2048]{2,1,0:T(8,128)(2,1)}, u32[]{:S(2)}, u32[]{:S(2)}) async-start(bf16[128,10,2048]{2,1,0:T(8,128)(2,1)} %reshape.81), calls=%async_computation | async-start | bytes 16777216 | tf_op jit(solution)/shard_map/all_to_all | solution.py:28
  35.6 9.6 %select_reduce_fusion = f32[1280]{0:T(1024)S(1)} fusion(f32[128,8]{0,1:T(8,128)S(1)} %copy-done.5, s32[128,8]{0,1:T(8,128)S(1)} %multiply_add_fusion), kind=kLoop, calls=%fused_computation.11 | loop fusion | flops 3930880 | bytes 13312 | tf_op jit(solution)/shard_map/reduce_sum | solution.py:47
  50.2 9.5 %reshape.86 = bf16[128,10,2048]{2,1,0:T(8,128)(2,1)} reshape(bf16[1280,2048]{1,0:T(8,128)(2,1)} %multiply_convert_fusion) | data formatting | bytes 10485760 | tf_op jit(solution)/shard_map/reshape | solution.py:54
  59.7 78.4 %all-to-all-done = bf16[128,10,2048]{2,1,0:T(8,128)(2,1)} async-done(((bf16[128,10,2048]{2,1,0:T(8,128)(2,1)}), bf16[128,10,2048]{2,1,0:T(8,128)(2,1)}, u32[]{:S(2)}, u32[]{:S(2)}) %all-to-all-start) | async-done | bytes 5242912 | tf_op jit(solution)/shard_map/all_to_all | solution.py:28
  138.1 8.1 %all-to-all-start.2 = ((bf16[128,10,2048]{2,1,0:T(8,128)(2,1)}), bf16[128,10,2048]{2,1,0:T(8,128)(2,1)}, u32[]{:S(2)}, u32[]{:S(2)}) async-start(bf16[128,10,2048]{2,1,0:T(8,128)(2,1)} %reshape.86), calls=%async_computation.2 | async-start | bytes 16777216 | tf_op jit(solution)/shard_map/all_to_all | solution.py:28
  146.2 9.8 %reshape.82 = bf16[1280,2048]{1,0:T(8,128)(2,1)} reshape(bf16[128,10,2048]{2,1,0:T(8,128)(2,1)} %all-to-all-done) | data formatting | bytes 10485760 | tf_op jit(solution)/shard_map/reshape | solution.py:60
  156.1 9.7 %fusion.9 = f32[1280,768]{1,0:T(8,128)} fusion(bf16[1280,2048]{1,0:T(8,128)(2,1)} %reshape.82, bf16[1,2048,768]{2,1,0:T(8,128)(2,1)} %param.14), kind=kOutput, calls=%fused_computation.28 | convolution fusion | flops 4026531840 | bytes 12320768 | tf_op jit(solution)/shard_map/dot_general | solution.py:9
  171.9 76.9 %all-to-all-done.2 = bf16[128,10,2048]{2,1,0:T(8,128)(2,1)} async-done(((bf16[128,10,2048]{2,1,0:T(8,128)(2,1)}), bf16[128,10,2048]{2,1,0:T(8,128)(2,1)}, u32[]{:S(2)}, u32[]{:S(2)}) %all-to-all-start.2) | async-done | bytes 5242912 | tf_op jit(solution)/shard_map/all_to_all | solution.py:28
  248.8 9.8 %reshape.87 = bf16[1280,2048]{1,0:T(8,128)(2,1)} reshape(bf16[128,10,2048]{2,1,0:T(8,128)(2,1)} %all-to-all-done.2) | data formatting | bytes 10485760 | tf_op jit(solution)/shard_map/reshape | solution.py:61
  258.7 10.6 %multiply_convert_fusion.1 = (bf16[1280,768]{1,0:T(8,128)(2,1)}, bf16[1280,768]{1,0:T(8,128)(2,1)}, bf16[1280,768]{1,0:T(8,128)(2,1)S(1)}) fusion(f32[1280,768]{1,0:T(8,128)} %fusion.13, f32[1280,768]{1,0:T(8,128)} %fusion.9, bf16[1280,2048]{1,0:T(8,128)(2,1)} %reshape.87, bf16[1,768,2048]{2,1,0:T(8,128)(2,1)S(1)} %copy-done), kind=kOutput, calls=%fused_computation.16 | convolution fusion | flops 4041277440 | bytes 22151168 | tf_op jit(solution)/shard_map/dot_general | solution.py:14
  276.6 9.5 %reshape.83 = bf16[128,10,2048]{2,1,0:T(8,128)(2,1)} reshape(bf16[1280,2048]{1,0:T(8,128)(2,1)} %convolution_convert_fusion) | data formatting | bytes 10485760 | tf_op jit(solution)/shard_map/reshape | solution.py:66
  286.1 17.2 %all-to-all-start.1 = ((bf16[128,10,2048]{2,1,0:T(8,128)(2,1)}), bf16[128,10,2048]{2,1,0:T(8,128)(2,1)}, u32[]{:S(2)}, u32[]{:S(2)}) async-start(bf16[128,10,2048]{2,1,0:T(8,128)(2,1)} %reshape.83), calls=%async_computation.1 | async-start | bytes 16777216 | tf_op jit(solution)/shard_map/all_to_all | solution.py:28
  309.4 7.8 %add_convert_fusion = bf16[1280,2048]{1,0:T(8,128)(2,1)} fusion(f32[1280,2048]{1,0:T(8,128)S(1)} %fusion.11, bf16[1280,768]{1,0:T(8,128)(2,1)} %get-tuple-element.25, bf16[1,2048,768]{2,1,0:T(8,128)(2,1)S(1)} %copy-done.8), kind=kOutput, calls=%fused_computation.4 | convolution fusion | flops 4031774720 | bytes 20840448 | tf_op jit(solution)/shard_map/dot_general | solution.py:22
  317.2 9.5 %reshape.88 = bf16[128,10,2048]{2,1,0:T(8,128)(2,1)} reshape(bf16[1280,2048]{1,0:T(8,128)(2,1)} %add_convert_fusion) | data formatting | bytes 10485760 | tf_op jit(solution)/shard_map/reshape | solution.py:67
  326.8 76.8 %all-to-all-done.1 = bf16[128,10,2048]{2,1,0:T(8,128)(2,1)} async-done(((bf16[128,10,2048]{2,1,0:T(8,128)(2,1)}), bf16[128,10,2048]{2,1,0:T(8,128)(2,1)}, u32[]{:S(2)}, u32[]{:S(2)}) %all-to-all-start.1) | async-done | bytes 5242912 | tf_op jit(solution)/shard_map/all_to_all | solution.py:28
  403.6 9.1 %all-to-all-start.3 = ((bf16[128,10,2048]{2,1,0:T(8,128)(2,1)}), bf16[128,10,2048]{2,1,0:T(8,128)(2,1)}, u32[]{:S(2)}, u32[]{:S(2)}) async-start(bf16[128,10,2048]{2,1,0:T(8,128)(2,1)} %reshape.88), calls=%async_computation.3 | async-start | bytes 16777216 | tf_op jit(solution)/shard_map/all_to_all | solution.py:28
  412.9 9.2 %fusion.17 = bf16[1,768,2048]{2,1,0:T(8,128)(2,1)} fusion(bf16[1280,768]{1,0:T(8,128)(2,1)} %copy-done.9, bf16[1280,2048]{1,0:T(8,128)(2,1)} %reshape.87), kind=kOutput, calls=%fused_computation.36 | convolution fusion | flops 4028104704 | bytes 10354688 | tf_op jit(solution)/shard_map/dot_general | solution.py:15
  422.1 8.5 %fusion.16 = bf16[1,2048,768]{2,1,0:T(8,128)(2,1)} fusion(bf16[1280,2048]{1,0:T(8,128)(2,1)} %reshape.82, bf16[1280,768]{1,0:T(8,128)(2,1)S(1)} %copy-done.11), kind=kOutput, calls=%fused_computation.35 | convolution fusion | flops 4028104704 | bytes 10354688 | tf_op jit(solution)/shard_map/dot_general | solution.py:19
  436.3 9.8 %reshape.84 = bf16[1280,2048]{1,0:T(8,128)(2,1)} reshape(bf16[128,10,2048]{2,1,0:T(8,128)(2,1)} %all-to-all-done.1) | data formatting | bytes 10485760 | tf_op jit(solution)/shard_map/reshape | solution.py:68
  446.2 12.0 %gather_fusion = bf16[1024,2048]{1,0:T(8,128)(2,1)} fusion(bf16[1280,2048]{1,0:T(8,128)(2,1)} %reshape.84, s32[1024]{0:T(1024)S(1)} %broadcast_clamp_fusion), kind=kCustom, calls=%fused_computation.clone | custom fusion | bytes 8392704 | tf_op jit(solution)/shard_map/jit(_take)/gather | solution.py:68
  468.7 46.5 %all-to-all-done.3 = bf16[128,10,2048]{2,1,0:T(8,128)(2,1)} async-done(((bf16[128,10,2048]{2,1,0:T(8,128)(2,1)}), bf16[128,10,2048]{2,1,0:T(8,128)(2,1)}, u32[]{:S(2)}, u32[]{:S(2)}) %all-to-all-start.3) | async-done | bytes 5242912 | tf_op jit(solution)/shard_map/all_to_all | solution.py:28
  515.2 9.8 %reshape.89 = bf16[1280,2048]{1,0:T(8,128)(2,1)} reshape(bf16[128,10,2048]{2,1,0:T(8,128)(2,1)} %all-to-all-done.3) | data formatting | bytes 10485760 | tf_op jit(solution)/shard_map/reshape | solution.py:72
  525.0 12.2 %gather_fusion.1 = bf16[1024,2048]{1,0:T(8,128)(2,1)} fusion(bf16[1280,2048]{1,0:T(8,128)(2,1)} %reshape.89, s32[1024]{0:T(1024)S(1)} %broadcast_clamp_fusion), kind=kCustom, calls=%fused_computation.1.clone | custom fusion | bytes 8392704 | tf_op jit(solution)/shard_map/jit(_take)/gather | solution.py:72
  (59 shorter events, 60.2 us)
Async XLA Ops:
  0.6 258.0 %copy-start = (bf16[1,768,2048]{2,1,0:T(8,128)(2,1)S(1)}, bf16[1,768,2048]{2,1,0:T(8,128)(2,1)}, u32[]{:S(2)}) copy-start(bf16[1,768,2048]{2,1,0:T(8,128)(2,1)} %param.15) | copy-start | bytes 9437188
  2.1 0.8 copy-start.3
  24.4 11.3 %copy-start.5 = (f32[128,8]{0,1:T(8,128)S(1)}, f32[128,8]{0,1:T(8,128)}, u32[]{:S(2)}) copy-start(f32[128,8]{0,1:T(8,128)} %param.12) | copy-start | bytes 12292
  24.4 113.8 %all-to-all-start = ((bf16[128,10,2048]{2,1,0:T(8,128)(2,1)}), bf16[128,10,2048]{2,1,0:T(8,128)(2,1)}, u32[]{:S(2)}, u32[]{:S(2)}) async-start(bf16[128,10,2048]{2,1,0:T(8,128)(2,1)} %reshape.81), calls=%async_computation | async-start | bytes 16777216 | tf_op jit(solution)/shard_map/all_to_all | solution.py:28
  138.1 110.7 %all-to-all-start.2 = ((bf16[128,10,2048]{2,1,0:T(8,128)(2,1)}), bf16[128,10,2048]{2,1,0:T(8,128)(2,1)}, u32[]{:S(2)}, u32[]{:S(2)}) async-start(bf16[128,10,2048]{2,1,0:T(8,128)(2,1)} %reshape.86), calls=%async_computation.2 | async-start | bytes 16777216 | tf_op jit(solution)/shard_map/all_to_all | solution.py:28
  156.0 9.7 %copy-start.2 = (bf16[1280,2048]{1,0:T(8,128)(2,1)S(1)}, bf16[1280,2048]{1,0:T(8,128)(2,1)}, u32[]{:S(2)}) copy-start(bf16[1280,2048]{1,0:T(8,128)(2,1)} %reshape.82) | copy-start | bytes 15728644
  156.0 9.7 %copy-start.6 = (bf16[1,2048,768]{2,1,0:T(8,128)(2,1)S(1)}, bf16[1,2048,768]{2,1,0:T(8,128)(2,1)}, u32[]{:S(2)}) copy-start(bf16[1,2048,768]{2,1,0:T(8,128)(2,1)} %param.13) | copy-start | bytes 9437188
  269.2 1.3 copy-start.9
  286.1 17.2 %copy-start.7 = (bf16[1,2048,768]{2,1,0:T(8,128)(2,1)S(1)}, bf16[1,2048,768]{2,1,0:T(8,128)(2,1)}, u32[]{:S(2)}) copy-start(bf16[1,2048,768]{2,1,0:T(8,128)(2,1)} %param.13) | copy-start | bytes 9437188
  286.1 117.4 %all-to-all-start.1 = ((bf16[128,10,2048]{2,1,0:T(8,128)(2,1)}), bf16[128,10,2048]{2,1,0:T(8,128)(2,1)}, u32[]{:S(2)}, u32[]{:S(2)}) async-start(bf16[128,10,2048]{2,1,0:T(8,128)(2,1)} %reshape.83), calls=%async_computation.1 | async-start | bytes 16777216 | tf_op jit(solution)/shard_map/all_to_all | solution.py:28
  303.3 6.1 %copy-start.8 = (bf16[1,2048,768]{2,1,0:T(8,128)(2,1)S(1)}, bf16[1,2048,768]{2,1,0:T(8,128)(2,1)}, u32[]{:S(2)}) copy-start(bf16[1,2048,768]{2,1,0:T(8,128)(2,1)} %param.14) | copy-start | bytes 9437188
  326.8 85.9 %copy-start.4 = (bf16[128,2048]{1,0:T(8,128)(2,1)S(1)}, bf16[128,2048]{1,0:T(8,128)(2,1)}, u32[]{:S(2)}) copy-start(bf16[128,2048]{1,0:T(8,128)(2,1)} %param.10) | copy-start | bytes 1572868
  403.6 111.6 %all-to-all-start.3 = ((bf16[128,10,2048]{2,1,0:T(8,128)(2,1)}), bf16[128,10,2048]{2,1,0:T(8,128)(2,1)}, u32[]{:S(2)}, u32[]{:S(2)}) async-start(bf16[128,10,2048]{2,1,0:T(8,128)(2,1)} %reshape.88), calls=%async_computation.3 | async-start | bytes 16777216 | tf_op jit(solution)/shard_map/all_to_all | solution.py:28
  412.9 9.2 %copy-start.11 = (bf16[1280,768]{1,0:T(8,128)(2,1)S(1)}, bf16[1280,768]{1,0:T(8,128)(2,1)}, u32[]{:S(2)}) copy-start(bf16[1280,768]{1,0:T(8,128)(2,1)} %get-tuple-element.25) | copy-start | bytes 5898244
  412.9 17.7 %slice-start = ((s8[5242880]{0:T(1024)(128)(4,1)}), s8[4194304]{0:T(1024)(128)(4,1)S(1)}, s32[]{:S(2)}) async-start(s8[5242880]{0:T(1024)(128)(4,1)} %bitcast.59), calls=%async_computation.4 | async-start | bytes 8388608
  422.1 8.5 %slice-start.1 = ((s8[5242880]{0:T(1024)(128)(4,1)}), s8[1048576]{0:T(1024)(128)(4,1)S(1)}, s32[]{:S(2)}) async-start(s8[5242880]{0:T(1024)(128)(4,1)} %bitcast.59), calls=%async_computation.5 | async-start | bytes 2097152
  422.1 8.5 %copy-start.10 = (bf16[1280,768]{1,0:T(8,128)(2,1)S(1)}, bf16[1280,768]{1,0:T(8,128)(2,1)}, u32[]{:S(2)}) copy-start(bf16[1280,768]{1,0:T(8,128)(2,1)} %get-tuple-element.26) | copy-start | bytes 5898244
  525.0 17.3 %copy-start.1 = (bf16[1,768,2048]{2,1,0:T(8,128)(2,1)S(1)}, bf16[1,768,2048]{2,1,0:T(8,128)(2,1)}, u32[]{:S(2)}) copy-start(bf16[1,768,2048]{2,1,0:T(8,128)(2,1)} %param.15) | copy-start | bytes 9437188
where the time goes:
time: 554 us; the launch traced here: 543 us
  waiting for transfers between devices  279 us (50%)
  local copies, waits for them, and re-layouts  106 us (19%)
  matrix products  79.5 us (14%)
  starting transfers between devices  45.6 us (8%)
  other arithmetic  31.6 us (6%)
    all_to_all x4, waiting for transfers between devices, travel_one(): lax.all_to_all(block, ('group', 'ingroup'), split_axis=0, concat_axis=0,...  279 us
    all_to_all x4, starting transfers between devices, travel_one(): lax.all_to_all(block, ('group', 'ingroup'), split_axis=0, concat_axis=0,...  45.6 us
    gather x1, local copies, waits for them, and re-layouts, body(): jnp.take(back_grad.reshape(flat_shape), slot_index, axis=0)  12.2 us
    gather x1, local copies, waits for them, and re-layouts, body(): jnp.take(back_out.reshape(flat_shape), slot_index, axis=0)  12 us
  transfers between devices with their start and end apart: 4, of which 4 were waited for; matrix products, arithmetic and copies ran while one was open for 24% of the time, Pallas kernels for 0%

commit v1 on v0

v1 whole, which is shorter than its diff:
```python
import functools

import jax
import jax.numpy as jnp
from jax import lax
from jax.experimental import pallas as pl
from jax.experimental.pallas import tpu as pltpu
from jax.sharding import PartitionSpec as P

MESH = pl.DeviceIdType.MESH
AXES = ("group", "ingroup")
PEERS = 128
CAP = 10
STRIDE = 37
UNSTRIDE = pow(STRIDE, -1, PEERS)
LANES = 128
VMEM_LIMIT = 56 * 1024 * 1024


def peer(j, sign):
    k = (j * STRIDE) % PEERS
    group, ingroup = lax.axis_index("group"), lax.axis_index("ingroup")
    core, z, x = ingroup % 2, (ingroup // 2) % 4, ingroup // 8
    dc, dz, dx, dy = k % 2, (k // 2) % 4, (k // 8) % 4, k // 32
    if sign < 0:
        dc, dz, dx, dy = 2 - dc, 4 - dz, 4 - dx, 4 - dy
    return (group + dy) % 4, (((x + dx) % 4) * 4 + (z + dz) % 4) * 2 + (core + dc) % 2


def relative(routes):
    group, ingroup = lax.axis_index("group"), lax.axis_index("ingroup")
    core, z, x = ingroup % 2, (ingroup // 2) % 4, ingroup // 8
    dy = (routes // 32 - group + 4) % 4
    dx = ((routes // 8) % 4 - x + 4) % 4
    dz = ((routes // 2) % 4 - z + 4) % 4
    dc = (routes % 2 - core + 2) % 2
    return ((dy * 32 + dx * 8 + dz * 2 + dc) * UNSTRIDE) % PEERS


def dispatch_kernel(source, gate, tokens, cotangent, x_in, u_in, x_out, u_out, x_send, u_send, x_recv, u_recv, own_sem):
    def one(j, carry):
        base = j * CAP
        for p in range(CAP):
            t = source[base + p]
            x_out[base + p] = tokens[t]
            u_out[base + p] = (gate[base + p] * cotangent[t].astype(jnp.float32)).astype(jnp.bfloat16)

        @pl.when(j > 0)
        def _():
            place = pl.ds(base, CAP)
            for src, dst, send, recv in ((x_out, x_in, x_send, x_recv), (u_out, u_in, u_send, u_recv)):
                pltpu.make_async_remote_copy(
                    src.at[place], dst.at[place], send, recv, device_id=peer(j, 1), device_id_type=MESH
                ).start()

        return carry

    lax.fori_loop(0, PEERS, one, 0)
    own = pl.ds(0, CAP)
    for src, dst in ((x_out, x_in), (u_out, u_in)):
        copy = pltpu.make_async_copy(src.at[own], dst.at[own], own_sem)
        copy.start()
        copy.wait()
    wait_all(x_out, x_in, x_send, x_recv)
    wait_all(u_out, u_in, u_send, u_recv)


def wait_all(src, dst, send, recv):
    others = pl.ds(CAP, (PEERS - 1) * CAP)
    every = pltpu.make_async_remote_copy(
        src.at[others], dst.at[others], send, recv,
        device_id=(lax.axis_index("group"), lax.axis_index("ingroup")), device_id_type=MESH,
    )
    every.wait_send()
    every.wait_recv()


def combine_kernel(slot, gate, out, grad, cotangent, mixed, grad_tokens, grad_gates, out_in, grad_in, o_send, g_send, o_recv, g_recv, own_sem):
    for src, dst, send, recv in ((out, out_in, o_send, o_recv), (grad, grad_in, g_send, g_recv)):
        def one(j, carry, src=src, dst=dst, send=send, recv=recv):
            place = pl.ds(j * CAP, CAP)
            pltpu.make_async_remote_copy(
                src.at[place], dst.at[place], send, recv, device_id=peer(j, -1), device_id_type=MESH
            ).start()
            return carry

        lax.fori_loop(1, PEERS, one, 0)
        own = pl.ds(0, CAP)
        copy = pltpu.make_async_copy(src.at[own], dst.at[own], own_sem)
        copy.start()
        copy.wait()
    tokens, choices = mixed.shape[0], grad_gates.shape[1]
    wait_all(out, out_in, o_send, o_recv)

    def mix(t, carry):
        cot = cotangent[t].astype(jnp.float32)
        total = jnp.zeros(cot.shape, jnp.float32)
        parts = []
        for k in range(choices):
            row = out_in[slot[t * choices + k]].astype(jnp.float32)
            total = total + gate[t * choices + k] * row
            parts.append(jnp.sum(row * cot, axis=0, keepdims=True))
        mixed[t] = total.astype(jnp.bfloat16)
        sums = jnp.sum(jnp.concatenate(parts, axis=0), axis=1, keepdims=True)
        grad_gates[t] = jnp.broadcast_to(sums, (choices, LANES))
        return carry

    lax.fori_loop(0, tokens, mix, 0)
    wait_all(grad, grad_in, g_send, g_recv)

    def add(t, carry):
        total = grad_in[slot[t * choices]].astype(jnp.float32)
        for k in range(1, choices):
            total = total + grad_in[slot[t * choices + k]].astype(jnp.float32)
        grad_tokens[t] = total.astype(jnp.bfloat16)
        return carry

    lax.fori_loop(0, tokens, add, 0)


def expert_pass(inputs, upstream, w_gate, w_up, w_down):
    gate_pre = jnp.dot(inputs, w_gate, preferred_element_type=jnp.float32)
    up_pre = jnp.dot(inputs, w_up, preferred_element_type=jnp.float32)
    sigmoid = jax.nn.sigmoid(gate_pre)
    swish = gate_pre * sigmoid
    hidden = (swish * up_pre).astype(jnp.bfloat16)
    output = jnp.dot(hidden, w_down, preferred_element_type=jnp.float32).astype(jnp.bfloat16)
    d_hidden = jnp.dot(upstream, w_down.T, preferred_element_type=jnp.float32)
    grad_down = jnp.dot(hidden.T, upstream, preferred_element_type=jnp.float32).astype(jnp.bfloat16)
    d_gate = (d_hidden * up_pre * sigmoid * (1.0 + gate_pre * (1.0 - sigmoid))).astype(jnp.bfloat16)
    d_up = (d_hidden * swish).astype(jnp.bfloat16)
    grad_gate = jnp.dot(inputs.T, d_gate, preferred_element_type=jnp.float32).astype(jnp.bfloat16)
    grad_up = jnp.dot(inputs.T, d_up, preferred_element_type=jnp.float32).astype(jnp.bfloat16)
    d_inputs = (
        jnp.dot(d_gate, w_gate.T, preferred_element_type=jnp.float32)
        + jnp.dot(d_up, w_up.T, preferred_element_type=jnp.float32)
    ).astype(jnp.bfloat16)
    return (output, d_inputs, grad_gate, grad_up, grad_down)


def plan(routes, gate_weights):
    order = relative(routes)
    onehot = order[:, :, None] == jnp.arange(PEERS, dtype=jnp.int32)[None, None, :]
    named = jnp.any(onehot, axis=1)
    weight = jnp.sum(jnp.where(onehot, gate_weights[:, :, None], 0.0), axis=1)
    count = routes.shape[0]
    lower = (jnp.arange(count)[:, None] >= jnp.arange(count)[None, :]).astype(jnp.bfloat16)
    upto = jnp.dot(lower, named.astype(jnp.bfloat16), preferred_element_type=jnp.float32).astype(jnp.int32)
    place = jnp.arange(CAP, dtype=jnp.int32)
    source = jnp.sum((upto[:, :, None] <= place).astype(jnp.int32), axis=0)
    taken = named[:, :, None] & (upto[:, :, None] - 1 == place)
    slot_gate = jnp.sum(jnp.where(taken, weight[:, :, None], 0.0), axis=0)
    position = jnp.sum(jnp.where(onehot, upto[:, None, :] - 1, 0), axis=2)
    return source.reshape(-1), slot_gate.reshape(-1), (order * CAP + position).reshape(-1)


def body(tokens, cotangent, routes, gate_weights, weight_gate, weight_up, weight_down):
    count, choices = routes.shape
    features = tokens.shape[1]
    tiles = features // LANES
    slots = PEERS * CAP
    source, slot_gate, slot = plan(routes, gate_weights)
    token_rows = jnp.pad(tokens.reshape(count, tiles, LANES), ((0, 8), (0, 0), (0, 0)))
    cot_rows = jnp.pad(cotangent.reshape(count, tiles, LANES), ((0, 8), (0, 0), (0, 0)))
    smem, vmem = pl.BlockSpec(memory_space=pltpu.SMEM), pl.BlockSpec(memory_space=pltpu.VMEM)
    hbm = pl.BlockSpec(memory_space=pl.ANY)
    slot_shape = jax.ShapeDtypeStruct((slots, tiles, LANES), jnp.bfloat16)
    semaphores = [pltpu.SemaphoreType.DMA] * 5
    x_in, u_in = pl.pallas_call(
        dispatch_kernel,
        out_shape=(slot_shape, slot_shape),
        in_specs=[smem, smem, vmem, vmem],
        out_specs=(hbm, hbm),
        scratch_shapes=[pltpu.VMEM(slot_shape.shape, jnp.bfloat16)] * 2 + semaphores,
        compiler_params=pltpu.CompilerParams(has_side_effects=True, vmem_limit_bytes=VMEM_LIMIT),
    )(source, slot_gate, token_rows, cot_rows)
    output, d_inputs, grad_gate, grad_up, grad_down = expert_pass(
        x_in.reshape(slots, features), u_in.reshape(slots, features), weight_gate[0], weight_up[0], weight_down[0]
    )
    row_shape = jax.ShapeDtypeStruct((count, tiles, LANES), jnp.bfloat16)
    mixed, grad_tokens, grad_gates = pl.pallas_call(
        combine_kernel,
        out_shape=(row_shape, row_shape, jax.ShapeDtypeStruct((count, choices, LANES), jnp.float32)),
        in_specs=[smem, smem, hbm, hbm, vmem],
        out_specs=(vmem, vmem, vmem),
        scratch_shapes=[pltpu.VMEM(slot_shape.shape, jnp.bfloat16)] * 2 + semaphores,
        compiler_params=pltpu.CompilerParams(has_side_effects=True, vmem_limit_bytes=VMEM_LIMIT),
    )(slot, gate_weights.reshape(-1), output.reshape(slot_shape.shape), d_inputs.reshape(slot_shape.shape), cot_rows)
    return (
        mixed.reshape(count, features),
        grad_tokens.reshape(count, features),
        grad_gates[:, :, 0],
        grad_gate[None],
        grad_up[None],
        grad_down[None],
    )


def solution(mesh):
    split2, split3 = P(AXES, None), P(AXES, None, None)
    return jax.shard_map(
        body,
        mesh=mesh,
        in_specs=(split2, split2, split2, split2, split3, split3, split3),
        out_specs=(split2, split2, split2, split3, split3, split3),
        check_vma=False,
    )
```

time: 554 us -> 387 us (0.70); the launches traced: 543 us -> 386 us
  Pallas kernels: 0 us -> 288 us
  waiting for transfers between devices: 279 us -> 0 us
  local copies, waits for them, and re-layouts: 106 us -> 21.5 us
  starting transfers between devices: 45.6 us -> 0 us
  other arithmetic: 31.6 us -> 3.85 us
  matrix products: 79.5 us -> 71.9 us
    pallas_call x0 -> x2, Pallas kernels: none -> 288 us  [the longest x1 149 us: body(): pl.pallas_call(dispatch_kernel, out_shape=(slot_shape, slot_shape), in_sp...]
    all_to_all x4 -> x0, waiting for transfers between devices: 279 us -> none  [travel_one(): lax.all_to_all(block, ('group', 'ingroup'), split_axis=0, concat_axis=0,...]
    reshape x8 -> x5, local copies, waits for them, and re-layouts: 77.5 us -> 5.24 us  [the longest x1 2.4 us: body(): grad_tokens.reshape(count, features)]
    all_to_all x4 -> x0, starting transfers between devices: 45.6 us -> none  [travel_one(): lax.all_to_all(block, ('group', 'ingroup'), split_axis=0, concat_axis=0,...]
    gather x2 -> x0, local copies, waits for them, and re-layouts: 24.1 us -> none  [the longest x1 12.2 us: body(): jnp.take(back_grad.reshape(flat_shape), slot_index, axis=0)]
    reduce_sum x5 -> x4, other arithmetic: 24.8 us -> 2.95 us  [the longest x1 2.38 us: plan(): position = jnp.sum(jnp.where(onehot, upto[:, None, :] - 1, 0), axis=2)]
    dot_general x2 -> x1, matrix products: 9.79 us -> 0.15 us  [plan(): jnp.dot(lower, named.astype(jnp.bfloat16), preferred_element_type=jnp.flo...]
    unnamed x31 -> x28, local copies, waits for them, and re-layouts: 3.88 us -> 12.4 us
  transfers between devices with their start and end apart: 4 -> 0, of which waited for: 4 -> 0; matrix products, arithmetic and copies ran while one was open for 24% -> 0% of each run, Pallas kernels for 0% -> 0%
where the time goes in v1:
time: 387 us; the launch traced here: 386 us
  Pallas kernels  288 us (74%)
  matrix products  71.9 us (19%)
  local copies, waits for them, and re-layouts  21.5 us (6%)
    pallas_call x1, Pallas kernels, body(): pl.pallas_call(dispatch_kernel, out_shape=(slot_shape, slot_shape), in_sp...  149 us
    pallas_call x1, Pallas kernels, body(): pl.pallas_call(combine_kernel, out_shape=(row_shape, row_shape, jax.Shape...  139 us
    unnamed x28, local copies, waits for them, and re-layouts  12.4 us
    dot_general x1, matrix products, expert_pass(): jnp.dot(inputs.T, d_up, preferred_element_type=jnp.float32)  10.6 us
    dot_general x1, matrix products, expert_pass(): d_hidden = jnp.dot(upstream, w_down.T, preferred_element_type=jnp.float32)  9.56 us
    dot_general x1, matrix products, expert_pass(): jnp.dot(hidden.T, upstream, preferred_element_type=jnp.float32)  9.21 us
    dot_general x1, matrix products, expert_pass(): gate_pre = jnp.dot(inputs, w_gate, preferred_element_type=jnp.float32)  8.76 us
    dot_general x1, matrix products, expert_pass(): jnp.dot(d_gate, w_gate.T, preferred_element_type=jnp.float32)  8.3 us

profile of v1, /device:TPU:7, one launch (start us, length us, event | category | flops | bytes accessed | tf_op | source)
XLA Modules:
  0.0 385.7 jit_solution(10988675539599717106)
XLA Ops:
  0.7 0.9 copy.21
  2.4 0.8 copy.25
  3.8 0.7 reshape.60.gate
  4.7 0.7 reshape.59.source
  5.4 1.3 copy.31
  6.7 0.9 pad.8.cotangent
  7.7 1.1 copy.30
  8.8 0.9 pad.7.tokens
  9.7 148.9 %shard_map.118 = (bf16[1280,16,128]{2,1,0:T(8,128)(2,1)}, bf16[1280,16,128]{2,1,0:T(8,128)(2,1)}) custom-call(s32[1280]{0:T(1024)} %reshape.59.source, f32[1280]{0:T(1024)} %reshape.60.gate, bf16[136,16,128]{2,1,0:T(8,128)(2,1)} %pad.7.tokens, bf16[136,16,128]{2,1,0:T(8,128)(2,1)} %pad.8.cotangent), custom_call_target="tpu_custom_call" | custom-call | tf_op jit(solution)/shard_map/pallas_call | solution.py:169
  158.7 8.8 %fusion.10 = f32[1280,768]{1,0:T(8,128)} fusion(bf16[160,8,16,128]{3,2,1,0:T(8,128)(2,1)} %bitcast.92, bf16[1,2048,768]{2,1,0:T(8,128)(2,1)S(1)} %copy-done.2), kind=kOutput, calls=%fused_computation.12 | convolution fusion | flops 4026531840 | bytes 12320768 | tf_op jit(solution)/shard_map/dot_general | solution.py:122
  167.4 6.2 %fusion.8 = f32[1280,768]{1,0:T(8,128)} fusion(bf16[160,8,16,128]{3,2,1,0:T(8,128)(2,1)S(1)} %bitcast.94, bf16[1,2048,768]{2,1,0:T(8,128)(2,1)S(1)} %copy-done.3), kind=kOutput, calls=%fused_computation.10 | convolution fusion | flops 4026531840 | bytes 12320768 | tf_op jit(solution)/shard_map/dot_general | solution.py:123
  173.6 9.6 %multiply_convert_fusion = (bf16[1280,768]{1,0:T(8,128)(2,1)}, bf16[1280,768]{1,0:T(8,128)(2,1)}, bf16[1280,768]{1,0:T(8,128)(2,1)}) fusion(f32[1280,768]{1,0:T(8,128)} %fusion.10, f32[1280,768]{1,0:T(8,128)} %fusion.8, bf16[1,768,2048]{2,1,0:T(8,128)(2,1)S(1)} %copy-done, bf16[160,8,16,128]{3,2,1,0:T(8,128)(2,1)S(1)} %bitcast.101), kind=kOutput, calls=%fused_computation.16 | convolution fusion | flops 4041277440 | bytes 22151168 | tf_op jit(solution)/shard_map/dot_general | solution.py:128
  183.2 8.3 %fusion.32 = f32[1280,2048]{1,0:T(8,128)} fusion(bf16[1280,768]{1,0:T(8,128)(2,1)} %get-tuple-element.23, bf16[1,2048,768]{2,1,0:T(8,128)(2,1)S(1)} %copy-done.2), kind=kOutput, calls=%fused_computation.32 | convolution fusion | flops 4026531840 | bytes 15597568 | tf_op jit(solution)/shard_map/dot_general | solution.py:135
  191.5 7.6 %fusion.47 = bf16[160,8,16,128]{3,1,2,0:T(8,128)(2,1)S(1)} fusion(f32[1280,2048]{1,0:T(8,128)} %fusion.32, bf16[1280,768]{1,0:T(8,128)(2,1)} %get-tuple-element.22, bf16[1,2048,768]{2,1,0:T(8,128)(2,1)S(1)} %copy-done.3), kind=kOutput, calls=%fused_computation.39 | convolution fusion | flops 4031774720 | bytes 20840448 | tf_op jit(solution)/shard_map/dot_general | solution.py:136
  199.1 4.1 %copy.35 = bf16[160,8,16,128]{3,2,1,0:T(8,128)(2,1)} copy(bf16[160,8,16,128]{3,1,2,0:T(8,128)(2,1)S(1)} %fusion.47) | data formatting | bytes 10485760
  203.3 4.4 %fusion.44 = bf16[160,8,16,128]{3,1,2,0:T(8,128)(2,1)S(1)} fusion(bf16[1280,768]{1,0:T(8,128)(2,1)S(1)} %copy-done.5, bf16[1,768,2048]{2,1,0:T(8,128)(2,1)S(1)} %copy-done), kind=kOutput, calls=%fused_computation.38 | convolution fusion | flops 4029153280 | bytes 10354688 | tf_op jit(solution)/shard_map/dot_general | solution.py:127
  207.7 4.1 %copy.33 = bf16[160,8,16,128]{3,2,1,0:T(8,128)(2,1)} copy(bf16[160,8,16,128]{3,1,2,0:T(8,128)(2,1)S(1)} %fusion.44) | data formatting | bytes 10485760
  211.8 2.4 select_reduce_fusion.2
  215.9 138.7 %shard_map.119 = (bf16[128,16,128]{2,1,0:T(8,128)(2,1)}, bf16[128,16,128]{2,1,0:T(8,128)(2,1)}, f32[128,8,128]{2,1,0:T(8,128)}) custom-call(s32[1024]{0:T(1024)} %reshape.57.slot, f32[1024]{0:T(1024)} %reshape.58.gate, bf16[1280,16,128]{2,1,0:T(8,128)(2,1)} %bitcast.83, bf16[1280,16,128]{2,1,0:T(8,128)(2,1)} %bitcast.82, bf16[136,16,128]{2,1,0:T(8,128)(2,1)} %pad.8.cotangent), custom_call_target="tpu_custom_call" | custom-call | tf_op jit(solution)/shard_map/pallas_call | solution.py:181
  354.6 2.4 copy_bitcast_fusion
  357.0 1.8 copy.29
  358.8 9.2 %fusion.35 = bf16[1,768,2048]{2,1,0:T(8,128)(2,1)} fusion(bf16[1280,768]{1,0:T(8,128)(2,1)} %get-tuple-element.24, bf16[160,8,16,128]{3,2,1,0:T(8,128)(2,1)} %bitcast.98), kind=kOutput, calls=%fused_computation.35 | convolution fusion | flops 4028104704 | bytes 10354688 | tf_op jit(solution)/shard_map/dot_general | solution.py:129
  368.0 10.6 %fusion.38 = bf16[1,2048,768]{2,1,0:T(8,128)(2,1)} fusion(bf16[1280,768]{1,0:T(8,128)(2,1)S(1)} %copy-done.6, bf16[160,8,16,128]{3,2,1,0:T(8,128)(2,1)} %bitcast.93), kind=kOutput, calls=%fused_computation.36 | convolution fusion | flops 4028104704 | bytes 10354688 | tf_op jit(solution)/shard_map/dot_general | solution.py:133
  378.7 7.0 %fusion.41 = bf16[1,2048,768]{2,1,0:T(8,128)(2,1)} fusion(bf16[1280,768]{1,0:T(8,128)(2,1)S(1)} %copy-done.4, bf16[160,8,16,128]{3,2,1,0:T(8,128)(2,1)S(1)} %bitcast.97), kind=kOutput, calls=%fused_computation.37 | convolution fusion | flops 4028104704 | bytes 10354688 | tf_op jit(solution)/shard_map/dot_general | solution.py:132
  (35 shorter events, 3.3 us)
Async XLA Ops:
  0.6 173.0 %copy-start = (bf16[1,768,2048]{2,1,0:T(8,128)(2,1)S(1)}, bf16[1,768,2048]{2,1,0:T(8,128)(2,1)}, u32[]{:S(2)}) copy-start(bf16[1,768,2048]{2,1,0:T(8,128)(2,1)} %param.13) | copy-start | bytes 9437188
  5.4 153.2 %copy-start.2 = (bf16[1,2048,768]{2,1,0:T(8,128)(2,1)S(1)}, bf16[1,2048,768]{2,1,0:T(8,128)(2,1)}, u32[]{:S(2)}) copy-start(bf16[1,2048,768]{2,1,0:T(8,128)(2,1)} %param.11) | copy-start | bytes 9437188
  158.6 8.8 %copy-start.1 = (bf16[1280,16,128]{2,1,0:T(8,128)(2,1)S(1)}, bf16[1280,16,128]{2,1,0:T(8,128)(2,1)}, u32[]{:S(2)}) copy-start(bf16[1280,16,128]{2,1,0:T(8,128)(2,1)} %get-tuple-element.11) | copy-start | bytes 15728644
  158.6 8.8 %copy-start.3 = (bf16[1,2048,768]{2,1,0:T(8,128)(2,1)S(1)}, bf16[1,2048,768]{2,1,0:T(8,128)(2,1)}, u32[]{:S(2)}) copy-start(bf16[1,2048,768]{2,1,0:T(8,128)(2,1)} %param.12) | copy-start | bytes 9437188
  158.6 15.0 %slice-start.2 = ((s8[5242880]{0:T(1024)(128)(4,1)}), s8[4194304]{0:T(1024)(128)(4,1)S(1)}, s32[]{:S(2)}) async-start(s8[5242880]{0:T(1024)(128)(4,1)} %bitcast.99), calls=%async_computation.2 | async-start | bytes 8388608
  167.4 6.2 %slice-start.3 = ((s8[5242880]{0:T(1024)(128)(4,1)}), s8[1048576]{0:T(1024)(128)(4,1)S(1)}, s32[]{:S(2)}) async-start(s8[5242880]{0:T(1024)(128)(4,1)} %bitcast.99), calls=%async_computation.3 | async-start | bytes 2097152
  199.1 4.2 %copy-start.5 = (bf16[1280,768]{1,0:T(8,128)(2,1)S(1)}, bf16[1280,768]{1,0:T(8,128)(2,1)}, u32[]{:S(2)}) copy-start(bf16[1280,768]{1,0:T(8,128)(2,1)} %get-tuple-element.24) | copy-start | bytes 5898244
  358.8 9.2 %copy-start.6 = (bf16[1280,768]{1,0:T(8,128)(2,1)S(1)}, bf16[1280,768]{1,0:T(8,128)(2,1)}, u32[]{:S(2)}) copy-start(bf16[1280,768]{1,0:T(8,128)(2,1)} %get-tuple-element.22) | copy-start | bytes 5898244
  358.8 19.9 %slice-start = ((s8[5242880]{0:T(1024)(128)(4,1)}), s8[4194304]{0:T(1024)(128)(4,1)S(1)}, s32[]{:S(2)}) async-start(s8[5242880]{0:T(1024)(128)(4,1)} %bitcast.95), calls=%async_computation | async-start | bytes 8388608
  368.0 10.7 %slice-start.1 = ((s8[5242880]{0:T(1024)(128)(4,1)}), s8[1048576]{0:T(1024)(128)(4,1)S(1)}, s32[]{:S(2)}) async-start(s8[5242880]{0:T(1024)(128)(4,1)} %bitcast.95), calls=%async_computation.1 | async-start | bytes 2097152
  368.0 10.7 %copy-start.4 = (bf16[1280,768]{1,0:T(8,128)(2,1)S(1)}, bf16[1280,768]{1,0:T(8,128)(2,1)}, u32[]{:S(2)}) copy-start(bf16[1280,768]{1,0:T(8,128)(2,1)} %get-tuple-element.23) | copy-start | bytes 5898244

commit v2 on v1

v2 whole, which is shorter than its diff:
```python
import functools

import jax
import jax.numpy as jnp
from jax import lax
from jax.experimental import pallas as pl
from jax.experimental.pallas import tpu as pltpu
from jax.sharding import PartitionSpec as P

MESH = pl.DeviceIdType.MESH
AXES = ("group", "ingroup")
PEERS = 128
CAP = 10
STRIDE = 37
UNSTRIDE = pow(STRIDE, -1, PEERS)
LANES = 128
VMEM_LIMIT = 63 * 1024 * 1024
CHUNKS = 4
BLOCKS = PEERS // CHUNKS
ROWS = BLOCKS * CAP
GROUP = 16
WIDE = 256


def peer(j, sign):
    k = (j * STRIDE) % PEERS
    group, ingroup = lax.axis_index("group"), lax.axis_index("ingroup")
    core, z, x = ingroup % 2, (ingroup // 2) % 4, ingroup // 8
    dc, dz, dx, dy = k % 2, (k // 2) % 4, (k // 8) % 4, k // 32
    if sign < 0:
        dc, dz, dx, dy = 2 - dc, 4 - dz, 4 - dx, 4 - dy
    return (group + dy) % 4, (((x + dx) % 4) * 4 + (z + dz) % 4) * 2 + (core + dc) % 2


def relative(routes):
    group, ingroup = lax.axis_index("group"), lax.axis_index("ingroup")
    core, z, x = ingroup % 2, (ingroup // 2) % 4, ingroup // 8
    dy = (routes // 32 - group + 4) % 4
    dx = ((routes // 8) % 4 - x + 4) % 4
    dz = ((routes // 2) % 4 - z + 4) % 4
    dc = (routes % 2 - core + 2) % 2
    return ((dy * 32 + dx * 8 + dz * 2 + dc) * UNSTRIDE) % PEERS


def to_rows(native):
    tiles = native.shape[1] // LANES
    return jnp.swapaxes(jnp.stack([native[:, c * LANES : (c + 1) * LANES] for c in range(tiles)]), 0, 1)


def rows_to_native(rows, native, start):
    columns = jnp.swapaxes(rows, 0, 1)
    for c in range(columns.shape[0]):
        native[pl.ds(start, GROUP), c * LANES : (c + 1) * LANES] = columns[c]


def loop(count, step):
    def one(i, carry):
        step(i)
        return carry

    lax.fori_loop(0, count, one, 0)


def here():
    return (lax.axis_index("group"), lax.axis_index("ingroup"))


def wait_sent(block, sem):
    pltpu.make_async_remote_copy(block, block, sem, sem, device_id=here(), device_id_type=MESH).wait_send()


def wait_arrived(block, sem):
    pltpu.make_async_remote_copy(block, block, sem, sem, device_id=here(), device_id_type=MESH).wait_recv()


def dot(a, b, dims):
    return lax.dot_general(a, b, (dims, ((), ())), preferred_element_type=jnp.float32)


NN, NT, TN = ((1,), (0,)), ((1,), (1,)), ((0,), (0,))


def layer_kernel(
    source, slot_gate, slot, gate, tokens, cotangent, w_gate_hbm, w_up_hbm, w_down_hbm,
    mixed, grad_tokens, grad_gates, g_gate, g_up, g_down,
    token_rows, cot_rows, x_out, u_out, x_in, u_in, o_back, d_back, x, u, w_gate, w_up, w_down, hidden, d_pre, native,
    stage_pre, stage_down, sum_rows,
    w_sem, x_send, u_send, x_recv, u_recv, o_send, d_send, o_recv, d_recv, own_sem, stage_sem,
):
    weights = [
        pltpu.make_async_copy(src, dst, w_sem.at[i])
        for i, (src, dst) in enumerate(((w_gate_hbm, w_gate), (w_up_hbm, w_up), (w_down_hbm, w_down)))
    ]
    for copy in weights:
        copy.start()
    count, features = tokens.shape
    inner = hidden.shape[1]

    def spread(i):
        at = pl.ds(pl.multiple_of(i * GROUP, GROUP), GROUP)
        token_rows[at] = to_rows(tokens[at, :])
        cot_rows[at] = to_rows(cotangent[at, :])

    loop(count // GROUP, spread)
    token_rows[count] = jnp.zeros(token_rows.shape[1:], jnp.bfloat16)
    cot_rows[count] = jnp.zeros(cot_rows.shape[1:], jnp.bfloat16)

    def send(chunk):
        ring = lax.rem(chunk, 2)

        def one(b):
            base = b * CAP
            first = chunk * ROWS + base
            for p in range(CAP):
                t = source[first + p]
                x_out[ring, base + p] = token_rows[t]
                u_out[ring, base + p] = (slot_gate[first + p] * cot_rows[t].astype(jnp.float32)).astype(jnp.bfloat16)
            j = chunk * BLOCKS + b
            moves = ((x_out, x_in, x_send, x_recv), (u_out, u_in, u_send, u_recv))

            @pl.when(j > 0)
            def _():
                for src, dst, sent, arrived in moves:
                    pltpu.make_async_remote_copy(
                        src.at[ring, pl.ds(base, CAP)], dst.at[chunk, pl.ds(base, CAP)], sent.at[ring], arrived.at[chunk],
                        device_id=peer(j, 1), device_id_type=MESH,
                    ).start()

            @pl.when(j == 0)
            def _():
                for i, (src, dst, sent, arrived) in enumerate(moves):
                    copy = pltpu.make_async_copy(src.at[0, pl.ds(0, CAP)], dst.at[0, pl.ds(0, CAP)], own_sem.at[i])
                    copy.start()
                    copy.wait()

        loop(BLOCKS, one)

    def rest(ref, chunk, act):
        @pl.when(chunk == 0)
        def _():
            act(ref.at[0, pl.ds(CAP, ROWS - CAP)])

        @pl.when(chunk > 0)
        def _():
            act(ref.at[1, pl.ds(0, ROWS)])

    def give_back(src, dst, sent, arrived, chunk):
        def one(b):
            j = chunk * BLOCKS + b
            at = pl.ds(b * CAP, CAP)

            @pl.when(j > 0)
            def _():
                pltpu.make_async_remote_copy(
                    src.at[chunk, at], dst.at[chunk, at], sent.at[chunk], arrived.at[chunk],
                    device_id=peer(j, -1), device_id_type=MESH,
                ).start()

            @pl.when(j == 0)
            def _():
                copy = pltpu.make_async_copy(src.at[0, pl.ds(0, CAP)], dst.at[0, pl.ds(0, CAP)], own_sem.at[0])
                copy.start()
                copy.wait()

        loop(BLOCKS, one)

    def chunk_rows(chunk):
        return pl.ds(pl.multiple_of(chunk * ROWS, ROWS), ROWS)

    def work(chunk):
        for src, arrived, dst in ((x_in, x_recv, x), (u_in, u_recv, u)):
            rest(src, chunk, lambda block, arrived=arrived: wait_arrived(block, arrived.at[chunk]))

            def unpack(i, src=src, dst=dst):
                start = pl.multiple_of(i * GROUP, GROUP)
                rows_to_native(src[chunk, pl.ds(start, GROUP)], dst, pl.multiple_of(chunk * ROWS + start, GROUP))

            loop(ROWS // GROUP, unpack)
        at = chunk_rows(chunk)

        @pl.when(chunk == 0)
        def _():
            for copy in weights:
                copy.wait()

        def first(n):
            cols = pl.ds(pl.multiple_of(n * WIDE, WIDE), WIDE)
            gate_pre = dot(x[at, :], w_gate[:, cols], NN)
            up_pre = dot(x[at, :], w_up[:, cols], NN)
            sigmoid = jax.nn.sigmoid(gate_pre)
            swish = gate_pre * sigmoid
            hidden[at, cols] = (swish * up_pre).astype(jnp.bfloat16)
            d_hidden = dot(u[at, :], w_down[cols, :], NT)
            d_gate = d_hidden * up_pre * sigmoid * (1.0 + gate_pre * (1.0 - sigmoid))
            d_pre[at, cols] = d_gate.astype(jnp.bfloat16)
            d_pre[at, pl.ds(pl.multiple_of(inner + n * WIDE, WIDE), WIDE)] = (d_hidden * swish).astype(jnp.bfloat16)

        loop(inner // WIDE, first)

        def pack(dst):
            def one(i):
                rows = pl.ds(pl.multiple_of(i * GROUP, GROUP), GROUP)
                dst[chunk, rows] = to_rows(native[rows, :])

            loop(ROWS // GROUP, one)

        def output(n):
            cols = pl.ds(pl.multiple_of(n * WIDE, WIDE), WIDE)
            native[:, cols] = dot(hidden[at, :], w_down[:, cols], NN).astype(jnp.bfloat16)

        loop(features // WIDE, output)
        pack(x_in)
        give_back(x_in, o_back, o_send, o_recv, chunk)

        def backward(n):
            cols = pl.ds(pl.multiple_of(n * WIDE, WIDE), WIDE)
            native[:, cols] = (
                dot(d_pre[at, :inner], w_gate[cols, :], NT) + dot(d_pre[at, inner:], w_up[cols, :], NT)
            ).astype(jnp.bfloat16)

        loop(features // WIDE, backward)
        pack(u_in)

    send(0)
    send(1)

    def step(chunk):
        work(chunk)

        @pl.when(chunk < CHUNKS - 2)
        def _():
            rest(x_out, chunk, lambda block: wait_sent(block, x_send.at[lax.rem(chunk, 2)]))
            rest(u_out, chunk, lambda block: wait_sent(block, u_send.at[lax.rem(chunk, 2)]))
            send(chunk + 2)

    loop(CHUNKS, step)
    loop(CHUNKS, lambda chunk: give_back(u_in, d_back, d_send, d_recv, chunk))

    pre_tiles = features // WIDE

    def grad_pre(i):
        ring = lax.rem(i, 2)
        rows = pl.ds(pl.multiple_of(i * WIDE, WIDE), WIDE)
        copies = lambda: [
            pltpu.make_async_copy(stage_pre.at[ring, half], out.at[rows, :], stage_sem.at[ring, half])
            for half, out in enumerate((g_gate, g_up))
        ]

        @pl.when(i >= 2)
        def _():
            for copy in copies():
                copy.wait()

        for half in range(2):
            stage_pre[ring, half] = dot(x[:, rows], d_pre[:, half * inner : (half + 1) * inner], TN).astype(jnp.bfloat16)
        for copy in copies():
            copy.start()

    loop(pre_tiles, grad_pre)
    for ring in range(2):
        for half, out in enumerate((g_gate, g_up)):
            pltpu.make_async_copy(stage_pre.at[ring, half], out.at[pl.ds(0, WIDE), :], stage_sem.at[ring, half]).wait()

    half_features = features // 2

    def grad_down(i):
        rows = pl.ds(pl.multiple_of(i * WIDE, WIDE), WIDE)
        for half in range(2):
            cols = pl.ds(half * half_features, half_features)
            copy = pltpu.make_async_copy(stage_down.at[half], g_down.at[rows, cols], stage_sem.at[2, half])

            @pl.when(i >= 1)
            def _(copy=copy):
                copy.wait()

            stage_down[half] = dot(hidden[:, rows], u[:, cols], TN).astype(jnp.bfloat16)
            copy.start()

    loop(inner // WIDE, grad_down)
    for half in range(2):
        pltpu.make_async_copy(
            stage_down.at[half], g_down.at[pl.ds(0, WIDE), pl.ds(half * half_features, half_features)], stage_sem.at[2, half]
        ).wait()

    choices = grad_gates.shape[1]

    def wait_back(back, arrived):
        loop(CHUNKS, lambda chunk: rest(back, chunk, lambda block: wait_arrived(block, arrived.at[chunk])))

    def pick(back, t, k):
        s = slot[t * choices + k]
        return back[s // ROWS, lax.rem(s, ROWS)].astype(jnp.float32)

    wait_back(o_back, o_recv)

    def mix(i):
        def one(r):
            t = i * GROUP + r
            cot = cot_rows[t].astype(jnp.float32)
            total = jnp.zeros(cot.shape, jnp.float32)
            parts = []
            for k in range(choices):
                row = pick(o_back, t, k)
                total = total + gate[t * choices + k] * row
                parts.append(jnp.sum(row * cot, axis=0, keepdims=True))
            sum_rows[r] = total.astype(jnp.bfloat16)
            sums = jnp.sum(jnp.concatenate(parts, axis=0), axis=1, keepdims=True)
            grad_gates[t] = jnp.broadcast_to(sums, (choices, LANES))

        loop(GROUP, one)
        rows_to_native(sum_rows[...], mixed, pl.multiple_of(i * GROUP, GROUP))

    loop(count // GROUP, mix)
    wait_back(d_back, d_recv)

    def add(i):
        def one(r):
            t = i * GROUP + r
            total = pick(d_back, t, 0)
            for k in range(1, choices):
                total = total + pick(d_back, t, k)
            sum_rows[r] = total.astype(jnp.bfloat16)

        loop(GROUP, one)
        rows_to_native(sum_rows[...], grad_tokens, pl.multiple_of(i * GROUP, GROUP))

    loop(count // GROUP, add)

    for ref, sem in ((x_out, x_send), (u_out, u_send)):
        for ring in range(2):
            wait_sent(ref.at[ring], sem.at[ring])
    for ref, sem in ((x_in, o_send), (u_in, d_send)):
        loop(CHUNKS, lambda chunk, ref=ref, sem=sem: rest(ref, chunk, lambda block: wait_sent(block, sem.at[chunk])))


def plan(routes, gate_weights):
    order = relative(routes)
    onehot = order[:, :, None] == jnp.arange(PEERS, dtype=jnp.int32)[None, None, :]
    named = jnp.any(onehot, axis=1)
    weight = jnp.sum(jnp.where(onehot, gate_weights[:, :, None], 0.0), axis=1)
    count = routes.shape[0]
    lower = (jnp.arange(count)[:, None] >= jnp.arange(count)[None, :]).astype(jnp.bfloat16)
    upto = jnp.dot(lower, named.astype(jnp.bfloat16), preferred_element_type=jnp.float32).astype(jnp.int32)
    place = jnp.arange(CAP, dtype=jnp.int32)
    source = jnp.sum((upto[:, :, None] <= place).astype(jnp.int32), axis=0)
    taken = named[:, :, None] & (upto[:, :, None] - 1 == place)
    slot_gate = jnp.sum(jnp.where(taken, weight[:, :, None], 0.0), axis=0)
    position = jnp.sum(jnp.where(onehot, upto[:, None, :] - 1, 0), axis=2)
    return source.reshape(-1), slot_gate.reshape(-1), (order * CAP + position).reshape(-1)


def body(tokens, cotangent, routes, gate_weights, weight_gate, weight_up, weight_down):
    count, choices = routes.shape
    features, inner = weight_gate.shape[1:]
    tiles = features // LANES
    slots = PEERS * CAP
    source, slot_gate, slot = plan(routes, gate_weights)
    smem, vmem = pl.BlockSpec(memory_space=pltpu.SMEM), pl.BlockSpec(memory_space=pltpu.VMEM)
    hbm = pl.BlockSpec(memory_space=pl.ANY)
    bf16 = jnp.bfloat16
    semaphore = pltpu.SemaphoreType.DMA
    mixed, grad_tokens, grad_gates, grad_gate, grad_up, grad_down = pl.pallas_call(
        layer_kernel,
        out_shape=(
            jax.ShapeDtypeStruct(tokens.shape, bf16),
            jax.ShapeDtypeStruct(tokens.shape, bf16),
            jax.ShapeDtypeStruct((count, choices, LANES), jnp.float32),
            jax.ShapeDtypeStruct((features, inner), bf16),
            jax.ShapeDtypeStruct((features, inner), bf16),
            jax.ShapeDtypeStruct((inner, features), bf16),
        ),
        in_specs=[smem] * 4 + [vmem] * 2 + [hbm] * 3,
        out_specs=(vmem, vmem, vmem, hbm, hbm, hbm),
        scratch_shapes=[
            pltpu.VMEM((count + 8, tiles, LANES), bf16),
            pltpu.VMEM((count + 8, tiles, LANES), bf16),
            pltpu.VMEM((2, ROWS, tiles, LANES), bf16),
            pltpu.VMEM((2, ROWS, tiles, LANES), bf16),
            pltpu.VMEM((CHUNKS, ROWS, tiles, LANES), bf16),
            pltpu.VMEM((CHUNKS, ROWS, tiles, LANES), bf16),
            pltpu.VMEM((CHUNKS, ROWS, tiles, LANES), bf16),
            pltpu.VMEM((CHUNKS, ROWS, tiles, LANES), bf16),
            pltpu.VMEM((slots, features), bf16),
            pltpu.VMEM((slots, features), bf16),
            pltpu.VMEM((features, inner), bf16),
            pltpu.VMEM((features, inner), bf16),
            pltpu.VMEM((inner, features), bf16),
            pltpu.VMEM((slots, inner), bf16),
            pltpu.VMEM((slots, 2 * inner), bf16),
            pltpu.VMEM((ROWS, features), bf16),
            pltpu.VMEM((2, 2, WIDE, inner), bf16),
            pltpu.VMEM((2, WIDE, features // 2), bf16),
            pltpu.VMEM((GROUP, tiles, LANES), bf16),
            semaphore((3,)),
            semaphore((2,)),
            semaphore((2,)),
            semaphore((CHUNKS,)),
            semaphore((CHUNKS,)),
            semaphore((CHUNKS,)),
            semaphore((CHUNKS,)),
            semaphore((CHUNKS,)),
            semaphore((CHUNKS,)),
            semaphore((2,)),
            semaphore((3, 2)),
        ],
        compiler_params=pltpu.CompilerParams(has_side_effects=True, vmem_limit_bytes=VMEM_LIMIT),
        cost_estimate=pl.CostEstimate(
            flops=18 * slots * features * inner, bytes_accessed=12 * features * inner, transcendentals=slots * inner
        ),
    )(source, slot_gate, slot, gate_weights.reshape(-1), tokens, cotangent, weight_gate[0], weight_up[0], weight_down[0])
    return (mixed, grad_tokens, grad_gates[:, :, 0], grad_gate[None], grad_up[None], grad_down[None])


def solution(mesh):
    split2, split3 = P(AXES, None), P(AXES, None, None)
    return jax.shard_map(
        body,
        mesh=mesh,
        in_specs=(split2, split2, split2, split2, split3, split3, split3),
        out_specs=(split2, split2, split2, split3, split3, split3),
        check_vma=False,
    )
```

time: 387 us -> 318 us (0.82)
  the two profiles are of different devices: /device:TPU:7 before, /device:TPU:20 now
where the time goes in v2:
time: 318 us
  Pallas kernels  295 us (93%)
  local copies, waits for them, and re-layouts  18.8 us (6%)
  other arithmetic  3.85 us (1%)
    pallas_call x1, Pallas kernels, body(): pl.pallas_call(layer_kernel, out_shape=(jax.ShapeDtypeStruct(tokens.shape...  295 us
    unnamed x11, local copies, waits for them, and re-layouts  13.9 us

profile of v2, /device:TPU:20, one launch (start us, length us, event | category | flops | bytes accessed | tf_op | source)
XLA Modules:
  0.0 318.1 jit_solution(15870542569712171840)
XLA Ops:
  0.7 0.8 copy.21
  1.5 0.3 add_select_fusion
  1.8 0.3 fusion.1
  2.0 0.8 copy.26
  2.8 0.7 reshape.36.gate
  3.5 0.3 select_reduce_fusion.2
  3.9 0.1 broadcast_add_fusion
  4.0 0.1 select_reduce_fusion
  4.2 0.1 convert_reduce_fusion
  4.2 2.4 select_reduce_fusion.1
  6.6 0.3 multiply_add_fusion
  7.0 0.7 reshape.35.slot
  7.7 0.1 copy.25
  7.8 0.7 reshape.33.source
  8.5 0.1 copy.27
  8.6 0.7 reshape.34.slot_gate
  9.3 294.6 %shard_map.118 = (bf16[128,2048]{1,0:T(8,128)(2,1)}, bf16[128,2048]{1,0:T(8,128)(2,1)}, f32[128,8,128]{2,1,0:T(8,128)}, bf16[2048,768]{1,0:T(8,128)(2,1)}, bf16[...) custom-call(s32[1280]{0:T(1024)} %reshape.33.source, f32[1280]{0:T(1024)} %reshape.34.slot_gate, s32[1024]{0:T(1024)} %reshape.35.slot, ...), custom_call_target="tpu_custom_call" | custom-call | flops 36238786560 | bytes 18874368 | tf_op jit(solution)/shard_map/pallas_call | solution.py:362
  303.9 1.8 copy.29
  305.8 1.9 copy.35
  307.6 1.9 copy.36
  309.5 3.9 %copy.37 = bf16[1,2048,768]{2,1,0:T(8,128)(2,1)} copy(bf16[1,2048,768]{2,1,0:T(8,128)(2,1)} %bitcast.11) | data formatting | bytes 6291456
  313.4 1.7 copy.38
  315.1 1.4 copy-done
  316.5 1.7 copy.39
  (3 shorter events, 0.0 us)
Async XLA Ops:
  309.5 3.9 %copy-start.1 = (bf16[2048,768]{1,0:T(8,128)(2,1)S(1)}, bf16[2048,768]{1,0:T(8,128)(2,1)}, u32[]{:S(2)}) copy-start(bf16[2048,768]{1,0:T(8,128)(2,1)} %get-tuple-element.16) | copy-start | bytes 9437188
  313.4 3.0 copy-start

commit v3 on v2

v3 whole, which is shorter than its diff:
```python
import functools

import jax
import jax.numpy as jnp
from jax import lax
from jax.experimental import pallas as pl
from jax.experimental.pallas import tpu as pltpu
from jax.sharding import PartitionSpec as P

MESH = pl.DeviceIdType.MESH
AXES = ("group", "ingroup")
PEERS = 128
CAP = 10
STRIDE = 37
UNSTRIDE = pow(STRIDE, -1, PEERS)
LANES = 128
VMEM_LIMIT = 63 * 1024 * 1024
CHUNKS = 4
BLOCKS = PEERS // CHUNKS
ROWS = BLOCKS * CAP
GROUP = 16
WIDE = 256


def peer(j, sign):
    k = (j * STRIDE) % PEERS
    group, ingroup = lax.axis_index("group"), lax.axis_index("ingroup")
    core, z, x = ingroup % 2, (ingroup // 2) % 4, ingroup // 8
    dc, dz, dx, dy = k % 2, (k // 2) % 4, (k // 8) % 4, k // 32
    if sign < 0:
        dc, dz, dx, dy = 2 - dc, 4 - dz, 4 - dx, 4 - dy
    return (group + dy) % 4, (((x + dx) % 4) * 4 + (z + dz) % 4) * 2 + (core + dc) % 2


def relative(routes):
    group, ingroup = here()
    core, z, x = ingroup % 2, (ingroup // 2) % 4, ingroup // 8
    dy = (routes // 32 + (4 - group)) % 4
    dx = (routes // 8 + (4 - x)) % 4
    dz = (routes // 2 + (4 - z)) % 4
    dc = (routes + (2 - core)) % 2
    return ((dy * 32 + dx * 8 + dz * 2 + dc) * UNSTRIDE) % PEERS


def to_rows(native):
    tiles = native.shape[1] // LANES
    return jnp.swapaxes(jnp.stack([native[:, c * LANES : (c + 1) * LANES] for c in range(tiles)]), 0, 1)


def rows_to_native(rows, native, start):
    columns = jnp.swapaxes(rows, 0, 1)
    for c in range(columns.shape[0]):
        native[pl.ds(start, GROUP), c * LANES : (c + 1) * LANES] = columns[c]


def loop(count, step):
    def one(i, carry):
        step(i)
        return carry

    lax.fori_loop(0, count, one, 0)


def here():
    return (lax.axis_index("group"), lax.axis_index("ingroup"))


def wait_sent(block, sem):
    pltpu.make_async_remote_copy(block, block, sem, sem, device_id=here(), device_id_type=MESH).wait_send()


def wait_arrived(block, sem):
    pltpu.make_async_remote_copy(block, block, sem, sem, device_id=here(), device_id_type=MESH).wait_recv()


def greet():
    barrier = pltpu.get_barrier_semaphore()

    def one(j):
        pl.semaphore_signal(barrier, inc=1, device_id=peer(j + 1, 1), device_id_type=MESH)

    loop(PEERS - 1, one)


def dot(a, b, dims):
    return lax.dot_general(a, b, (dims, ((), ())), preferred_element_type=jnp.float32)


NN, NT, TN = ((1,), (0,)), ((1,), (1,)), ((0,), (0,))


def plan(routes, gates, source, weight, slot):
    choices, count = routes.shape
    order = relative(routes[...])
    peers = lax.broadcasted_iota(jnp.int32, (PEERS, count), 0)
    named = jnp.zeros((PEERS, count), jnp.float32)
    weights = jnp.zeros((PEERS, count), jnp.float32)
    for k in range(choices):
        same = order[k : k + 1, :] == peers
        named = jnp.where(same, 1.0, named)
        weights = jnp.where(same, gates[k : k + 1, :], weights)
    weight[...] = weights
    earlier = lax.broadcasted_iota(jnp.int32, (count, count), 0) <= lax.broadcasted_iota(jnp.int32, (count, count), 1)
    upto = dot(named.astype(jnp.bfloat16), jnp.where(earlier, 1.0, 0.0).astype(jnp.bfloat16), NN)
    ones = jnp.ones((8, count), jnp.bfloat16)
    for p in range(CAP):
        before = jnp.where(upto <= p, 1.0, 0.0).astype(jnp.bfloat16)
        source[p : p + 1, :] = jnp.clip(dot(ones, before, NT)[:1].astype(jnp.int32), 0, count)
    for k in range(choices):
        at = jnp.sum(jnp.where(order[k : k + 1, :] == peers, upto, 0.0), axis=0, keepdims=True)
        slot[k : k + 1, :] = jnp.clip(order[k : k + 1, :] * CAP + at.astype(jnp.int32) - 1, 0, PEERS * CAP - 1)


def layer_kernel(
    routes, gates, tokens, cotangent, w_gate_hbm, w_up_hbm, w_down_hbm,
    mixed, grad_tokens, grad_gates, g_gate, g_up, g_down, o_back,
    token_rows, cot_rows, x_out, u_out, x_in, u_in, d_back, x, u, w_gate, w_up, w_down, hidden, d_pre, native,
    stage_pre, stage_down, parts, source_v, weight_v, slot_v, source, weight, slot, gate,
    w_sem, x_send, u_send, x_recv, u_recv, o_send, d_send, o_recv, d_recv, own_sem, stage_sem, table_sem,
):
    greet()
    weights = [
        pltpu.make_async_copy(src, dst, w_sem.at[i])
        for i, (src, dst) in enumerate(((w_gate_hbm, w_gate), (w_up_hbm, w_up), (w_down_hbm, w_down)))
    ]
    for copy in weights:
        copy.start()
    count, features = tokens.shape
    inner = hidden.shape[1]
    plan(routes, gates, source_v, weight_v, slot_v)
    tables = [
        pltpu.make_async_copy(src, dst, table_sem.at[i])
        for i, (src, dst) in enumerate(((source_v, source), (weight_v, weight), (slot_v, slot), (gates, gate)))
    ]
    for copy in tables:
        copy.start()

    def spread(i):
        at = pl.ds(pl.multiple_of(i * GROUP, GROUP), GROUP)
        token_rows[at] = to_rows(tokens[at, :])
        cot_rows[at] = to_rows(cotangent[at, :])

    loop(count // GROUP, spread)
    token_rows[count] = jnp.zeros(token_rows.shape[1:], jnp.bfloat16)
    cot_rows[count] = jnp.zeros(cot_rows.shape[1:], jnp.bfloat16)

    for copy in tables:
        copy.wait()
    pl.semaphore_wait(pltpu.get_barrier_semaphore(), PEERS - 1)

    def send(fill, src, dst, sent, arrived):
        def one(j):
            chunk, b = j // BLOCKS, j % BLOCKS
            at = pl.ds(b * CAP, CAP)
            for p in range(CAP):
                src[chunk, b * CAP + p] = fill(source[p, j], j)

            @pl.when(j > 0)
            def _():
                pltpu.make_async_remote_copy(
                    src.at[chunk, at], dst.at[chunk, at], sent.at[chunk], arrived.at[chunk],
                    device_id=peer(j, 1), device_id_type=MESH,
                ).start()

            @pl.when(j == 0)
            def _():
                copy = pltpu.make_async_copy(src.at[0, pl.ds(0, CAP)], dst.at[0, pl.ds(0, CAP)], own_sem.at[0])
                copy.start()
                copy.wait()

        loop(PEERS, one)

    def scaled(t, j):
        return (weight[j, jnp.minimum(t, count - 1)] * cot_rows[t].astype(jnp.float32)).astype(jnp.bfloat16)

    send(lambda t, j: token_rows[t], x_out, x_in, x_send, x_recv)
    send(scaled, u_out, u_in, u_send, u_recv)

    def rest(ref, chunk, act):
        @pl.when(chunk == 0)
        def _():
            act(ref.at[0, pl.ds(CAP, ROWS - CAP)])

        @pl.when(chunk > 0)
        def _():
            act(ref.at[1, pl.ds(0, ROWS)])

    def give_back(src, dst, sent, arrived, chunk):
        def one(b):
            j = chunk * BLOCKS + b
            at = pl.ds(b * CAP, CAP)

            @pl.when(j > 0)
            def _():
                pltpu.make_async_remote_copy(
                    src.at[chunk, at], dst.at[chunk, at], sent.at[chunk], arrived.at[chunk],
                    device_id=peer(j, -1), device_id_type=MESH,
                ).start()

            @pl.when(j == 0)
            def _():
                copy = pltpu.make_async_copy(src.at[0, pl.ds(0, CAP)], dst.at[0, pl.ds(0, CAP)], own_sem.at[0])
                copy.start()
                copy.wait()

        loop(BLOCKS, one)

    def chunk_rows(chunk):
        return pl.ds(pl.multiple_of(chunk * ROWS, ROWS), ROWS)

    def take(src, arrived, dst, chunk):
        rest(src, chunk, lambda block: wait_arrived(block, arrived.at[chunk]))

        def unpack(i):
            start = pl.multiple_of(i * GROUP, GROUP)
            rows_to_native(src[chunk, pl.ds(start, GROUP)], dst, pl.multiple_of(chunk * ROWS + start, GROUP))

        loop(ROWS // GROUP, unpack)

    def pack(dst, chunk):
        def one(i):
            rows = pl.ds(pl.multiple_of(i * GROUP, GROUP), GROUP)
            dst[chunk, rows] = to_rows(native[rows, :])

        loop(ROWS // GROUP, one)

    def columns(n):
        return pl.ds(pl.multiple_of(n * WIDE, WIDE), WIDE)

    def forward(chunk):
        take(x_in, x_recv, x, chunk)
        at = chunk_rows(chunk)

        @pl.when(chunk == 0)
        def _():
            for copy in weights:
                copy.wait()

        def first(n):
            cols = columns(n)
            gate_pre = dot(x[at, :], w_gate[:, cols], NN)
            up_pre = dot(x[at, :], w_up[:, cols], NN)
            hidden[at, cols] = (gate_pre * jax.nn.sigmoid(gate_pre) * up_pre).astype(jnp.bfloat16)

        loop(inner // WIDE, first)

        def output(n):
            cols = columns(n)
            native[:, cols] = dot(hidden[at, :], w_down[:, cols], NN).astype(jnp.bfloat16)

        loop(features // WIDE, output)
        pack(x_in, chunk)
        give_back(x_in, o_back, o_send, o_recv, chunk)

    def backward(chunk):
        take(u_in, u_recv, u, chunk)
        at = chunk_rows(chunk)

        def first(n):
            cols = columns(n)
            gate_pre = dot(x[at, :], w_gate[:, cols], NN)
            up_pre = dot(x[at, :], w_up[:, cols], NN)
            sigmoid = jax.nn.sigmoid(gate_pre)
            d_hidden = dot(u[at, :], w_down[cols, :], NT)
            d_gate = d_hidden * up_pre * sigmoid * (1.0 + gate_pre * (1.0 - sigmoid))
            d_pre[at, cols] = d_gate.astype(jnp.bfloat16)
            d_up = d_hidden * (gate_pre * sigmoid)
            d_pre[at, pl.ds(pl.multiple_of(inner + n * WIDE, WIDE), WIDE)] = d_up.astype(jnp.bfloat16)

        loop(inner // WIDE, first)

        def second(n):
            cols = columns(n)
            native[:, cols] = (
                dot(d_pre[at, :inner], w_gate[cols, :], NT) + dot(d_pre[at, inner:], w_up[cols, :], NT)
            ).astype(jnp.bfloat16)

        loop(features // WIDE, second)
        pack(u_in, chunk)
        give_back(u_in, d_back, d_send, d_recv, chunk)

    loop(CHUNKS, forward)
    loop(CHUNKS, backward)

    pre_tiles = features // WIDE

    def grad_pre(i):
        ring = lax.rem(i, 2)
        rows = pl.ds(pl.multiple_of(i * WIDE, WIDE), WIDE)
        copies = lambda: [
            pltpu.make_async_copy(stage_pre.at[ring, half], out.at[rows, :], stage_sem.at[ring, half])
            for half, out in enumerate((g_gate, g_up))
        ]

        @pl.when(i >= 2)
        def _():
            for copy in copies():
                copy.wait()

        for half in range(2):
            stage_pre[ring, half] = dot(x[:, rows], d_pre[:, half * inner : (half + 1) * inner], TN).astype(jnp.bfloat16)
        for copy in copies():
            copy.start()

    loop(pre_tiles, grad_pre)
    for ring in range(2):
        for half, out in enumerate((g_gate, g_up)):
            pltpu.make_async_copy(stage_pre.at[ring, half], out.at[pl.ds(0, WIDE), :], stage_sem.at[ring, half]).wait()

    half_features = features // 2

    def grad_down(i):
        rows = pl.ds(pl.multiple_of(i * WIDE, WIDE), WIDE)
        for half in range(2):
            cols = pl.ds(half * half_features, half_features)
            copy = pltpu.make_async_copy(stage_down.at[half], g_down.at[rows, cols], stage_sem.at[2, half])

            @pl.when(i >= 1)
            def _(copy=copy):
                copy.wait()

            stage_down[half] = dot(hidden[:, rows], u[:, cols], TN).astype(jnp.bfloat16)
            copy.start()

    loop(inner // WIDE, grad_down)
    for half in range(2):
        pltpu.make_async_copy(
            stage_down.at[half], g_down.at[pl.ds(0, WIDE), pl.ds(half * half_features, half_features)], stage_sem.at[2, half]
        ).wait()

    choices = grad_gates.shape[0]

    def wait_back(back, arrived):
        loop(CHUNKS, lambda chunk: rest(back, chunk, lambda block: wait_arrived(block, arrived.at[chunk])))

    def pick(back, t, k):
        s = slot[k, t]
        return back[s // ROWS, lax.rem(s, ROWS)].astype(jnp.float32)

    wait_back(o_back, o_recv)
    loop(CHUNKS, lambda chunk: rest(x_out, chunk, lambda block: wait_sent(block, x_send.at[chunk])))
    landed = pltpu.make_async_copy(o_back, x_out, own_sem.at[1])
    landed.start()
    landed.wait()

    def mix(i):
        def one(r):
            t = i * GROUP + r
            cot = cot_rows[t].astype(jnp.float32)
            total = jnp.zeros(cot.shape, jnp.float32)
            for k in range(choices):
                row = pick(x_out, t, k)
                total = total + gate[k, t] * row
                parts[pl.ds(k * count + t, 1), :] = jnp.sum(row * cot, axis=0, keepdims=True)
            mixed[t] = total.astype(jnp.bfloat16)

        loop(GROUP, one)

    loop(count // GROUP, mix)
    for k in range(choices):
        grad_gates[k : k + 1, :] = jnp.sum(jnp.transpose(parts[k * count : (k + 1) * count, :]), axis=0, keepdims=True)
    wait_back(d_back, d_recv)

    def add(i):
        def one(r):
            t = i * GROUP + r
            total = pick(d_back, t, 0)
            for k in range(1, choices):
                total = total + pick(d_back, t, k)
            grad_tokens[t] = total.astype(jnp.bfloat16)

        loop(GROUP, one)

    loop(count // GROUP, add)

    for ref, sem in ((u_out, u_send), (x_in, o_send), (u_in, d_send)):
        loop(CHUNKS, lambda chunk, ref=ref, sem=sem: rest(ref, chunk, lambda block: wait_sent(block, sem.at[chunk])))


def body(tokens, cotangent, routes, gate_weights, weight_gate, weight_up, weight_down):
    count, choices = routes.shape
    features, inner = weight_gate.shape[1:]
    tiles = features // LANES
    slots = PEERS * CAP
    vmem = pl.BlockSpec(memory_space=pltpu.VMEM)
    hbm = pl.BlockSpec(memory_space=pl.ANY)
    bf16 = jnp.bfloat16
    semaphore = pltpu.SemaphoreType.DMA
    mixed, grad_tokens, grad_gates, grad_gate, grad_up, grad_down, _ = pl.pallas_call(
        layer_kernel,
        out_shape=(
            jax.ShapeDtypeStruct((count, tiles, LANES), bf16),
            jax.ShapeDtypeStruct((count, tiles, LANES), bf16),
            jax.ShapeDtypeStruct((choices, count), jnp.float32),
            jax.ShapeDtypeStruct((features, inner), bf16),
            jax.ShapeDtypeStruct((features, inner), bf16),
            jax.ShapeDtypeStruct((inner, features), bf16),
            jax.ShapeDtypeStruct((CHUNKS, ROWS, tiles, LANES), bf16),
        ),
        in_specs=[vmem] * 4 + [hbm] * 3,
        out_specs=(vmem, vmem, vmem, hbm, hbm, hbm, hbm),
        scratch_shapes=[
            pltpu.VMEM((count + 8, tiles, LANES), bf16),
            pltpu.VMEM((count + 8, tiles, LANES), bf16),
            pltpu.VMEM((CHUNKS, ROWS, tiles, LANES), bf16),
            pltpu.VMEM((CHUNKS, ROWS, tiles, LANES), bf16),
            pltpu.VMEM((CHUNKS, ROWS, tiles, LANES), bf16),
            pltpu.VMEM((CHUNKS, ROWS, tiles, LANES), bf16),
            pltpu.VMEM((CHUNKS, ROWS, tiles, LANES), bf16),
            pltpu.VMEM((slots, features), bf16),
            pltpu.VMEM((slots, features), bf16),
            pltpu.VMEM((features, inner), bf16),
            pltpu.VMEM((features, inner), bf16),
            pltpu.VMEM((inner, features), bf16),
            pltpu.VMEM((slots, inner), bf16),
            pltpu.VMEM((slots, 2 * inner), bf16),
            pltpu.VMEM((ROWS, features), bf16),
            pltpu.VMEM((2, 2, WIDE, inner), bf16),
            pltpu.VMEM((2, WIDE, features // 2), bf16),
            pltpu.VMEM((choices * count, LANES), jnp.float32),
            pltpu.VMEM((16, PEERS), jnp.int32),
            pltpu.VMEM((PEERS, count), jnp.float32),
            pltpu.VMEM((choices, count), jnp.int32),
            pltpu.SMEM((16, PEERS), jnp.int32),
            pltpu.SMEM((PEERS, count), jnp.float32),
            pltpu.SMEM((choices, count), jnp.int32),
            pltpu.SMEM((choices, count), jnp.float32),
            semaphore((3,)),
            semaphore((CHUNKS,)),
            semaphore((CHUNKS,)),
            semaphore((CHUNKS,)),
            semaphore((CHUNKS,)),
            semaphore((CHUNKS,)),
            semaphore((CHUNKS,)),
            semaphore((CHUNKS,)),
            semaphore((CHUNKS,)),
            semaphore((2,)),
            semaphore((3, 2)),
            semaphore((4,)),
        ],
        compiler_params=pltpu.CompilerParams(
            collective_id=0, has_side_effects=True, vmem_limit_bytes=VMEM_LIMIT
        ),
        cost_estimate=pl.CostEstimate(
            flops=18 * slots * features * inner, bytes_accessed=12 * features * inner, transcendentals=slots * inner
        ),
    )(routes.T, gate_weights.T, tokens, cotangent, weight_gate[0], weight_up[0], weight_down[0])
    return (mixed.reshape(tokens.shape), grad_tokens.reshape(tokens.shape), grad_gates.T, grad_gate[None], grad_up[None], grad_down[None])


def solution(mesh):
    split2, split3 = P(AXES, None), P(AXES, None, None)
    return jax.shard_map(
        body,
        mesh=mesh,
        in_specs=(split2, split2, split2, split2, split3, split3, split3),
        out_specs=(split2, split2, split2, split3, split3, split3),
        check_vma=False,
    )
```

time: 318 us -> 293 us (0.921)
  the two profiles are of different devices: /device:TPU:20 before, /device:TPU:7 now
where the time goes in v3:
time: 293 us; the launch traced here: 290 us
  Pallas kernels  278 us (95%)
  local copies, waits for them, and re-layouts  12.3 us (4%)
    pallas_call x1, Pallas kernels, body(): pl.pallas_call(layer_kernel, out_shape=(jax.ShapeDtypeStruct((count, tile...  278 us
    unnamed x8, local copies, waits for them, and re-layouts  9.87 us

profile of v3, /device:TPU:7, one launch (start us, length us, event | category | flops | bytes accessed | tf_op | source)
XLA Modules:
  0.0 290.4 jit_solution(967108067818285177)
XLA Ops:
  0.6 277.5 %shard_map.118 = (bf16[128,16,128]{2,1,0:T(8,128)(2,1)}, bf16[128,16,128]{2,1,0:T(8,128)(2,1)}, f32[8,128]{1,0:T(8,128)}, bf16[2048,768]{1,0:T(8,128)(2,1)}, bf1...) custom-call(s32[8,128]{1,0:T(8,128)} %bitcast.24, f32[8,128]{1,0:T(8,128)} %bitcast.25, ...), custom_call_target="tpu_custom_call" | custom-call | flops 36238786560 | bytes 18874368 | tf_op jit(solution)/shard_map/pallas_call | solution.py:389
  278.2 2.4 copy_bitcast_fusion
  280.6 1.3 copy.21
  281.8 0.0 copy-start.1
  281.8 3.9 %copy.22 = bf16[1,2048,768]{2,1,0:T(8,128)(2,1)} copy(bf16[1,2048,768]{2,1,0:T(8,128)(2,1)} %bitcast.17) | data formatting | bytes 6291456
  285.7 0.0 copy-done.1
  285.7 0.0 copy-start
  285.7 1.7 copy.23
  287.4 1.4 copy-done
  288.8 1.7 copy.24
Async XLA Ops:
  281.8 3.9 %copy-start.1 = (bf16[2048,768]{1,0:T(8,128)(2,1)S(1)}, bf16[2048,768]{1,0:T(8,128)(2,1)}, u32[]{:S(2)}) copy-start(bf16[2048,768]{1,0:T(8,128)(2,1)} %get-tuple-element.16) | copy-start | bytes 9437188
  285.7 3.0 %copy-start = (bf16[768,2048]{1,0:T(8,128)(2,1)S(1)}, bf16[768,2048]{1,0:T(8,128)(2,1)}, u32[]{:S(2)}) copy-start(bf16[768,2048]{1,0:T(8,128)(2,1)} %get-tuple-element.17) | copy-start | bytes 9437188

commit v4 on v3

--- a/solution.py
+++ b/solution.py
@@ -20,6 +20,7 @@
 ROWS = BLOCKS * CAP
 GROUP = 16
 WIDE = 256
+PIECES = 4
 
 
 def peer(j, sign):
@@ -113,9 +114,9 @@
 
 def layer_kernel(
     routes, gates, tokens, cotangent, w_gate_hbm, w_up_hbm, w_down_hbm,
-    mixed, grad_tokens, grad_gates, g_gate, g_up, g_down, o_back,
-    token_rows, cot_rows, x_out, u_out, x_in, u_in, d_back, x, u, w_gate, w_up, w_down, hidden, d_pre, native,
-    stage_pre, stage_down, parts, source_v, weight_v, slot_v, source, weight, slot, gate,
+    mixed, grad_gates, slot_v, g_gate, g_up, g_down, o_back, d_back,
+    token_rows, cot_rows, x_out, u_out, x_in, u_in, x, u, w_gate, w_up, w_down, hidden, d_pre, native,
+    stage_pre, stage_down, parts, source_v, weight_v, source, weight, slot, gate,
     w_sem, x_send, u_send, x_recv, u_recv, o_send, d_send, o_recv, d_recv, own_sem, stage_sem, table_sem,
 ):
     greet()
@@ -148,25 +149,29 @@
         copy.wait()
     pl.semaphore_wait(pltpu.get_barrier_semaphore(), PEERS - 1)
 
+    def block(j):
+        return pl.ds(j * CAP, CAP)
+
+    def move(src, dst, sent, arrived, j, sign):
+        @pl.when(j > 0)
+        def _():
+            chunk = j // BLOCKS
+            pltpu.make_async_remote_copy(
+                src.at[block(j)], dst.at[block(j)], sent.at[chunk], arrived.at[chunk],
+                device_id=peer(j, sign), device_id_type=MESH,
+            ).start()
+
+        @pl.when(j == 0)
+        def _():
+            copy = pltpu.make_async_copy(src.at[pl.ds(0, CAP)], dst.at[pl.ds(0, CAP)], own_sem.at[0])
+            copy.start()
+            copy.wait()
+
     def send(fill, src, dst, sent, arrived):
         def one(j):
-            chunk, b = j // BLOCKS, j % BLOCKS
-            at = pl.ds(b * CAP, CAP)
             for p in range(CAP):
-                src[chunk, b * CAP + p] = fill(source[p, j], j)
-
-            @pl.when(j > 0)
-            def _():
-                pltpu.make_async_remote_copy(
-                    src.at[chunk, at], dst.at[chunk, at], sent.at[chunk], arrived.at[chunk],
-                    device_id=peer(j, 1), device_id_type=MESH,
-                ).start()
-
-            @pl.when(j == 0)
-            def _():
-                copy = pltpu.make_async_copy(src.at[0, pl.ds(0, CAP)], dst.at[0, pl.ds(0, CAP)], own_sem.at[0])
-                copy.start()
-                copy.wait()
+                src[j * CAP + p] = fill(source[p, j], j)
+            move(src, dst, sent, arrived, j, 1)
 
         loop(PEERS, one)
 
@@ -179,31 +184,14 @@
     def rest(ref, chunk, act):
         @pl.when(chunk == 0)
         def _():
-            act(ref.at[0, pl.ds(CAP, ROWS - CAP)])
+            act(ref.at[pl.ds(CAP, ROWS - CAP)])
 
         @pl.when(chunk > 0)
         def _():
-            act(ref.at[1, pl.ds(0, ROWS)])
+            act(ref.at[pl.ds(ROWS, ROWS)])
 
     def give_back(src, dst, sent, arrived, chunk):
-        def one(b):
-            j = chunk * BLOCKS + b
-            at = pl.ds(b * CAP, CAP)
-
-            @pl.when(j > 0)
-            def _():
-                pltpu.make_async_remote_copy(
-                    src.at[chunk, at], dst.at[chunk, at], sent.at[chunk], arrived.at[chunk],
-                    device_id=peer(j, -1), device_id_type=MESH,
-                ).start()
-
-            @pl.when(j == 0)
-            def _():
-                copy = pltpu.make_async_copy(src.at[0, pl.ds(0, CAP)], dst.at[0, pl.ds(0, CAP)], own_sem.at[0])
-                copy.start()
-                copy.wait()
-
-        loop(BLOCKS, one)
+        loop(BLOCKS, lambda b: move(src, dst, sent, arrived, chunk * BLOCKS + b, -1))
 
     def chunk_rows(chunk):
         return pl.ds(pl.multiple_of(chunk * ROWS, ROWS), ROWS)
@@ -212,15 +200,15 @@
         rest(src, chunk, lambda block: wait_arrived(block, arrived.at[chunk]))
 
         def unpack(i):
-            start = pl.multiple_of(i * GROUP, GROUP)
-            rows_to_native(src[chunk, pl.ds(start, GROUP)], dst, pl.multiple_of(chunk * ROWS + start, GROUP))
+            start = pl.multiple_of(chunk * ROWS + i * GROUP, GROUP)
+            rows_to_native(src[pl.ds(start, GROUP)], dst, start)
 
         loop(ROWS // GROUP, unpack)
 
     def pack(dst, chunk):
         def one(i):
-            rows = pl.ds(pl.multiple_of(i * GROUP, GROUP), GROUP)
-            dst[chunk, rows] = to_rows(native[rows, :])
+            start = pl.multiple_of(i * GROUP, GROUP)
+            dst[pl.ds(chunk * ROWS + start, GROUP)] = to_rows(native[pl.ds(start, GROUP), :])
 
         loop(ROWS // GROUP, one)
 
@@ -334,8 +322,7 @@
         loop(CHUNKS, lambda chunk: rest(back, chunk, lambda block: wait_arrived(block, arrived.at[chunk])))
 
     def pick(back, t, k):
-        s = slot[k, t]
-        return back[s // ROWS, lax.rem(s, ROWS)].astype(jnp.float32)
+        return back[slot[k, t]].astype(jnp.float32)
 
     wait_back(o_back, o_recv)
     loop(CHUNKS, lambda chunk: rest(x_out, chunk, lambda block: wait_sent(block, x_send.at[chunk])))
@@ -361,20 +348,54 @@
         grad_gates[k : k + 1, :] = jnp.sum(jnp.transpose(parts[k * count : (k + 1) * count, :]), axis=0, keepdims=True)
     wait_back(d_back, d_recv)
 
-    def add(i):
-        def one(r):
-            t = i * GROUP + r
-            total = pick(d_back, t, 0)
-            for k in range(1, choices):
-                total = total + pick(d_back, t, k)
-            grad_tokens[t] = total.astype(jnp.bfloat16)
-
-        loop(GROUP, one)
-
-    loop(count // GROUP, add)
-
     for ref, sem in ((u_out, u_send), (x_in, o_send), (u_in, d_send)):
         loop(CHUNKS, lambda chunk, ref=ref, sem=sem: rest(ref, chunk, lambda block: wait_sent(block, sem.at[chunk])))
+
+
+def finish_kernel(
+    slot, d_back, mixed_rows, gates, g_gate, g_up, g_down, mixed, grad_tokens, grad_gates, out_gate, out_up, out_down,
+    back, sums, hold_gate, hold_up, hold_down, back_sem, in_sem, out_sem,
+):
+    landed = pltpu.make_async_copy(d_back, back, back_sem)
+    landed.start()
+    loads, stores = [], []
+    for i, (src, held, dst) in enumerate(
+        ((g_gate, hold_gate, out_gate), (g_up, hold_up, out_up), (g_down, hold_down, out_down))
+    ):
+        part = src.shape[0] // PIECES
+        for q in range(PIECES):
+            at = pl.ds(q * part, part)
+            loads.append(pltpu.make_async_copy(src.at[at], held.at[at], in_sem.at[i, q]))
+            stores.append(pltpu.make_async_copy(held.at[at], dst.at[at], out_sem.at[i, q]))
+    for copy in loads:
+        copy.start()
+    grad_gates[...] = gates[...]
+    count, choices = mixed.shape[0], slot.shape[0]
+
+    def spread(i):
+        start = pl.multiple_of(i * GROUP, GROUP)
+        rows_to_native(mixed_rows[pl.ds(start, GROUP)], mixed, start)
+
+    loop(count // GROUP, spread)
+    landed.wait()
+
+    def add(i):
+        start = pl.multiple_of(i * GROUP, GROUP)
+        for r in range(GROUP):
+            total = back[slot[0, start + r]].astype(jnp.float32)
+            for k in range(1, choices):
+                total = total + back[slot[k, start + r]].astype(jnp.float32)
+            sums[r] = total.astype(jnp.bfloat16)
+        rows_to_native(sums[...], grad_tokens, start)
+
+    half = count // GROUP // 2
+    loop(half, add)
+    for load, store in zip(loads, stores):
+        load.wait()
+        store.start()
+    loop(half, lambda i: add(half + i))
+    for copy in stores:
+        copy.wait()
 
 
 def body(tokens, cotangent, routes, gate_weights, weight_gate, weight_up, weight_down):
@@ -386,27 +407,32 @@
     hbm = pl.BlockSpec(memory_space=pl.ANY)
     bf16 = jnp.bfloat16
     semaphore = pltpu.SemaphoreType.DMA
-    mixed, grad_tokens, grad_gates, grad_gate, grad_up, grad_down, _ = pl.pallas_call(
+    weight_shapes = (
+        jax.ShapeDtypeStruct((features, inner), bf16),
+        jax.ShapeDtypeStruct((features, inner), bf16),
+        jax.ShapeDtypeStruct((inner, features), bf16),
+    )
+    gates_shape = jax.ShapeDtypeStruct((choices, count), jnp.float32)
+    slots_shape = jax.ShapeDtypeStruct((slots, tiles, LANES), bf16)
+    mixed, grad_gates, slot, grad_gate, grad_up, grad_down, _, d_back = pl.pallas_call(
         layer_kernel,
         out_shape=(
             jax.ShapeDtypeStruct((count, tiles, LANES), bf16),
-            jax.ShapeDtypeStruct((count, tiles, LANES), bf16),
-            jax.ShapeDtypeStruct((choices, count), jnp.float32),
-            jax.ShapeDtypeStruct((features, inner), bf16),
-            jax.ShapeDtypeStruct((features, inner), bf16),
-            jax.ShapeDtypeStruct((inner, features), bf16),
-            jax.ShapeDtypeStruct((CHUNKS, ROWS, tiles, LANES), bf16),
+            gates_shape,
+            jax.ShapeDtypeStruct((choices, count), jnp.int32),
+            *weight_shapes,
+            slots_shape,
+            slots_shape,
         ),
         in_specs=[vmem] * 4 + [hbm] * 3,
-        out_specs=(vmem, vmem, vmem, hbm, hbm, hbm, hbm),
+        out_specs=(vmem, vmem, vmem, hbm, hbm, hbm, hbm, hbm),
         scratch_shapes=[
             pltpu.VMEM((count + 8, tiles, LANES), bf16),
             pltpu.VMEM((count + 8, tiles, LANES), bf16),
-            pltpu.VMEM((CHUNKS, ROWS, tiles, LANES), bf16),
-            pltpu.VMEM((CHUNKS, ROWS, tiles, LANES), bf16),
-            pltpu.VMEM((CHUNKS, ROWS, tiles, LANES), bf16),
-            pltpu.VMEM((CHUNKS, ROWS, tiles, LANES), bf16),
-            pltpu.VMEM((CHUNKS, ROWS, tiles, LANES), bf16),
+            pltpu.VMEM((slots, tiles, LANES), bf16),
+            pltpu.VMEM((slots, tiles, LANES), bf16),
+            pltpu.VMEM((slots, tiles, LANES), bf16),
+            pltpu.VMEM((slots, tiles, LANES), bf16),
             pltpu.VMEM((slots, features), bf16),
             pltpu.VMEM((slots, features), bf16),
             pltpu.VMEM((features, inner), bf16),
@@ -420,7 +446,6 @@
             pltpu.VMEM((choices * count, LANES), jnp.float32),
             pltpu.VMEM((16, PEERS), jnp.int32),
             pltpu.VMEM((PEERS, count), jnp.float32),
-            pltpu.VMEM((choices, count), jnp.int32),
             pltpu.SMEM((16, PEERS), jnp.int32),
             pltpu.SMEM((PEERS, count), jnp.float32),
             pltpu.SMEM((choices, count), jnp.int32),
@@ -445,7 +470,31 @@
             flops=18 * slots * features * inner, bytes_accessed=12 * features * inner, transcendentals=slots * inner
         ),
     )(routes.T, gate_weights.T, tokens, cotangent, weight_gate[0], weight_up[0], weight_down[0])
-    return (mixed.reshape(tokens.shape), grad_tokens.reshape(tokens.shape), grad_gates.T, grad_gate[None], grad_up[None], grad_down[None])
+    smem = pl.BlockSpec(memory_space=pltpu.SMEM)
+    mixed, grad_tokens, grad_gates, grad_gate, grad_up, grad_down = pl.pallas_call(
+        finish_kernel,
+        out_shape=(
+            jax.ShapeDtypeStruct(tokens.shape, bf16),
+            jax.ShapeDtypeStruct(tokens.shape, bf16),
+            gates_shape,
+            *weight_shapes,
+        ),
+        in_specs=[smem, hbm, vmem, vmem, hbm, hbm, hbm],
+        out_specs=(vmem, vmem, vmem, hbm, hbm, hbm),
+        scratch_shapes=[
+            pltpu.VMEM((slots, tiles, LANES), bf16),
+            pltpu.VMEM((GROUP, tiles, LANES), bf16),
+            pltpu.VMEM((features, inner), bf16),
+            pltpu.VMEM((features, inner), bf16),
+            pltpu.VMEM((inner, features), bf16),
+            semaphore,
+            semaphore((3, PIECES)),
+            semaphore((3, PIECES)),
+        ],
+        compiler_params=pltpu.CompilerParams(vmem_limit_bytes=VMEM_LIMIT),
+        cost_estimate=pl.CostEstimate(flops=slots * features, bytes_accessed=12 * features * inner, transcendentals=0),
+    )(slot, d_back, mixed, grad_gates, grad_gate, grad_up, grad_down)
+    return (mixed, grad_tokens, grad_gates.T, grad_gate[None], grad_up[None], grad_down[None])
 
 
 def solution(mesh):

time: 293 us -> 282 us (0.962)
  the two profiles are of different devices: /device:TPU:7 before, /device:TPU:57 now
where the time goes in v4:
time: 282 us
  Pallas kernels  281 us (100%)
    pallas_call x1, Pallas kernels, body(): pl.pallas_call(layer_kernel, out_shape=(jax.ShapeDtypeStruct((count, tile...  270 us
    pallas_call x1, Pallas kernels, body(): pl.pallas_call(finish_kernel, out_shape=(jax.ShapeDtypeStruct(tokens.shap...  11.7 us

profile of v4, /device:TPU:57, one launch (start us, length us, event | category | flops | bytes accessed | tf_op | source)
XLA Modules:
  0.0 282.0 jit_solution(9298921607775208121)
XLA Ops:
  0.6 269.7 %shard_map.118 = (bf16[128,16,128]{2,1,0:T(8,128)(2,1)}, f32[8,128]{1,0:T(8,128)}, s32[8,128]{1,0:T(8,128)}, bf16[2048,768]{1,0:T(8,128)(2,1)}, bf16[2048,768]{1...) custom-call(s32[8,128]{1,0:T(8,128)} %bitcast.15, ...), custom_call_target="tpu_custom_call" | custom-call | flops 36238786560 | bytes 18874368 | tf_op jit(solution)/shard_map/pallas_call | solution.py:417
  270.3 11.7 %shard_map.119 = (bf16[128,2048]{1,0:T(8,128)(2,1)}, bf16[128,2048]{1,0:T(8,128)(2,1)}, f32[8,128]{1,0:T(8,128)}, bf16[2048,768]{1,0:T(8,128)(2,1)}, bf16[2048,7...) custom-call(s32[8,128]{1,0:T(8,128)} %get-tuple-element.19.slot, bf16[1280,16,128]{2,1,0:T(8,128)(2,1)} %get-tuple-element.20.d_back, ...), custom_call_target="tpu_custom_call" | custom-call | flops 2621440 | bytes 18874368 | tf_op jit(solution)/shard_map/pallas_call | solution.py:474

commit v5 on v4

--- a/solution.py
+++ b/solution.py
@@ -23,19 +23,22 @@
 PIECES = 4
 
 
+def position():
+    group, ingroup = here()
+    return group, lax.div(ingroup, 8), lax.rem(lax.div(ingroup, 2), 4), lax.rem(ingroup, 2)
+
+
 def peer(j, sign):
-    k = (j * STRIDE) % PEERS
-    group, ingroup = lax.axis_index("group"), lax.axis_index("ingroup")
-    core, z, x = ingroup % 2, (ingroup // 2) % 4, ingroup // 8
-    dc, dz, dx, dy = k % 2, (k // 2) % 4, (k // 8) % 4, k // 32
+    k = lax.rem(j * STRIDE, PEERS)
+    y, x, z, core = position()
+    dy, dx, dz, dc = lax.div(k, 32), lax.rem(lax.div(k, 8), 4), lax.rem(lax.div(k, 2), 4), lax.rem(k, 2)
     if sign < 0:
-        dc, dz, dx, dy = 2 - dc, 4 - dz, 4 - dx, 4 - dy
-    return (group + dy) % 4, (((x + dx) % 4) * 4 + (z + dz) % 4) * 2 + (core + dc) % 2
+        dy, dx, dz = 4 - dy, 4 - dx, 4 - dz
+    return (lax.rem(y + dy, 4), (lax.rem(x + dx, 4) * 4 + lax.rem(z + dz, 4)) * 2 + lax.rem(core + dc, 2))
 
 
 def relative(routes):
-    group, ingroup = here()
-    core, z, x = ingroup % 2, (ingroup // 2) % 4, ingroup // 8
+    group, x, z, core = position()
     dy = (routes // 32 + (4 - group)) % 4
     dx = (routes // 8 + (4 - x)) % 4
     dz = (routes // 2 + (4 - z)) % 4
@@ -76,11 +79,16 @@
 
 def greet():
     barrier = pltpu.get_barrier_semaphore()
-
-    def one(j):
-        pl.semaphore_signal(barrier, inc=1, device_id=peer(j + 1, 1), device_id_type=MESH)
-
-    loop(PEERS - 1, one)
+    y, x, z, core = position()
+    ys = [lax.rem(y + d, 4) for d in range(4)]
+    xs = [lax.rem(x + d, 4) * 8 for d in range(4)]
+    zs = [lax.rem(z + d, 4) * 2 for d in range(4)]
+    cores = [lax.rem(core + d, 2) for d in range(2)]
+    planes = [[a + b for b in zs] for a in xs]
+    for j in range(1, PEERS):
+        k = (j * STRIDE) % PEERS
+        device = (ys[k // 32], planes[(k // 8) % 4][(k // 2) % 4] + cores[k % 2])
+        pl.semaphore_signal(barrier, inc=1, device_id=device, device_id_type=MESH)
 
 
 def dot(a, b, dims):
@@ -114,9 +122,9 @@
 
 def layer_kernel(
     routes, gates, tokens, cotangent, w_gate_hbm, w_up_hbm, w_down_hbm,
-    mixed, grad_gates, slot_v, g_gate, g_up, g_down, o_back, d_back,
-    token_rows, cot_rows, x_out, u_out, x_in, u_in, x, u, w_gate, w_up, w_down, hidden, d_pre, native,
-    stage_pre, stage_down, parts, source_v, weight_v, source, weight, slot, gate,
+    mixed, grad_tokens, grad_gates, g_gate, g_up, g_down, o_back,
+    token_rows, cot_rows, x_out, u_out, x_in, u_in, d_back, x, u, w_gate, w_up, w_down, hidden, d_pre, native,
+    stage_pre, stage_down, parts, total, source_v, weight_v, slot_v, source, weight, slot, gate,
     w_sem, x_send, u_send, x_recv, u_recv, o_send, d_send, o_recv, d_recv, own_sem, stage_sem, table_sem,
 ):
     greet()
@@ -155,7 +163,7 @@
     def move(src, dst, sent, arrived, j, sign):
         @pl.when(j > 0)
         def _():
-            chunk = j // BLOCKS
+            chunk = lax.div(j, BLOCKS)
             pltpu.make_async_remote_copy(
                 src.at[block(j)], dst.at[block(j)], sent.at[chunk], arrived.at[chunk],
                 device_id=peer(j, sign), device_id_type=MESH,
@@ -346,18 +354,39 @@
     loop(count // GROUP, mix)
     for k in range(choices):
         grad_gates[k : k + 1, :] = jnp.sum(jnp.transpose(parts[k * count : (k + 1) * count, :]), axis=0, keepdims=True)
-    wait_back(d_back, d_recv)
+    total[...] = jnp.zeros(total.shape, jnp.float32)
+
+    def add(chunk):
+        rest(d_back, chunk, lambda block: wait_arrived(block, d_recv.at[chunk]))
+
+        def unpack(i):
+            start = pl.multiple_of(i * GROUP, GROUP)
+            rows_to_native(d_back[pl.ds(chunk * ROWS + start, GROUP)], native, start)
+
+        loop(ROWS // GROUP, unpack)
+        places = lax.broadcasted_iota(jnp.int32, (ROWS, count), 0) + chunk * ROWS
+        owner = jnp.zeros((ROWS, count), jnp.float32)
+        for k in range(choices):
+            owner = jnp.where(places == slot_v[k : k + 1, :], 1.0, owner)
+        owner = owner.astype(jnp.bfloat16)
+
+        def block_sum(n):
+            cols = columns(n)
+            total[:, cols] += dot(owner, native[:, cols], TN)
+
+        loop(features // WIDE, block_sum)
+
+    loop(CHUNKS, add)
+    grad_tokens[...] = total[...].astype(jnp.bfloat16)
 
     for ref, sem in ((u_out, u_send), (x_in, o_send), (u_in, d_send)):
         loop(CHUNKS, lambda chunk, ref=ref, sem=sem: rest(ref, chunk, lambda block: wait_sent(block, sem.at[chunk])))
 
 
 def finish_kernel(
-    slot, d_back, mixed_rows, gates, g_gate, g_up, g_down, mixed, grad_tokens, grad_gates, out_gate, out_up, out_down,
-    back, sums, hold_gate, hold_up, hold_down, back_sem, in_sem, out_sem,
+    mixed_rows, token_sums, gates, g_gate, g_up, g_down, mixed, grad_tokens, grad_gates, out_gate, out_up, out_down,
+    hold_gate, hold_up, hold_down, in_sem, out_sem,
 ):
-    landed = pltpu.make_async_copy(d_back, back, back_sem)
-    landed.start()
     loads, stores = [], []
     for i, (src, held, dst) in enumerate(
         ((g_gate, hold_gate, out_gate), (g_up, hold_up, out_up), (g_down, hold_down, out_down))
@@ -369,31 +398,17 @@
             stores.append(pltpu.make_async_copy(held.at[at], dst.at[at], out_sem.at[i, q]))
     for copy in loads:
         copy.start()
+    for load, store in zip(loads, stores):
+        load.wait()
+        store.start()
     grad_gates[...] = gates[...]
-    count, choices = mixed.shape[0], slot.shape[0]
+    grad_tokens[...] = token_sums[...]
 
     def spread(i):
         start = pl.multiple_of(i * GROUP, GROUP)
         rows_to_native(mixed_rows[pl.ds(start, GROUP)], mixed, start)
 
-    loop(count // GROUP, spread)
-    landed.wait()
-
-    def add(i):
-        start = pl.multiple_of(i * GROUP, GROUP)
-        for r in range(GROUP):
-            total = back[slot[0, start + r]].astype(jnp.float32)
-            for k in range(1, choices):
-                total = total + back[slot[k, start + r]].astype(jnp.float32)
-            sums[r] = total.astype(jnp.bfloat16)
-        rows_to_native(sums[...], grad_tokens, start)
-
-    half = count // GROUP // 2
-    loop(half, add)
-    for load, store in zip(loads, stores):
-        load.wait()
-        store.start()
-    loop(half, lambda i: add(half + i))
+    loop(mixed.shape[0] // GROUP, spread)
     for copy in stores:
         copy.wait()
 
@@ -414,21 +429,21 @@
     )
     gates_shape = jax.ShapeDtypeStruct((choices, count), jnp.float32)
     slots_shape = jax.ShapeDtypeStruct((slots, tiles, LANES), bf16)
-    mixed, grad_gates, slot, grad_gate, grad_up, grad_down, _, d_back = pl.pallas_call(
+    mixed, grad_tokens, grad_gates, grad_gate, grad_up, grad_down, _ = pl.pallas_call(
         layer_kernel,
         out_shape=(
             jax.ShapeDtypeStruct((count, tiles, LANES), bf16),
+            jax.ShapeDtypeStruct(tokens.shape, bf16),
             gates_shape,
-            jax.ShapeDtypeStruct((choices, count), jnp.int32),
             *weight_shapes,
-            slots_shape,
             slots_shape,
         ),
         in_specs=[vmem] * 4 + [hbm] * 3,
-        out_specs=(vmem, vmem, vmem, hbm, hbm, hbm, hbm, hbm),
+        out_specs=(vmem, vmem, vmem, hbm, hbm, hbm, hbm),
         scratch_shapes=[
             pltpu.VMEM((count + 8, tiles, LANES), bf16),
             pltpu.VMEM((count + 8, tiles, LANES), bf16),
+            pltpu.VMEM((slots, tiles, LANES), bf16),
             pltpu.VMEM((slots, tiles, LANES), bf16),
             pltpu.VMEM((slots, tiles, LANES), bf16),
             pltpu.VMEM((slots, tiles, LANES), bf16),
@@ -444,8 +459,10 @@
             pltpu.VMEM((2, 2, WIDE, inner), bf16),
             pltpu.VMEM((2, WIDE, features // 2), bf16),
             pltpu.VMEM((choices * count, LANES), jnp.float32),
+            pltpu.VMEM((count, features), jnp.float32),
             pltpu.VMEM((16, PEERS), jnp.int32),
             pltpu.VMEM((PEERS, count), jnp.float32),
+            pltpu.VMEM((choices, count), jnp.int32),
             pltpu.SMEM((16, PEERS), jnp.int32),
             pltpu.SMEM((PEERS, count), jnp.float32),
             pltpu.SMEM((choices, count), jnp.int32),
@@ -470,7 +487,6 @@
             flops=18 * slots * features * inner, bytes_accessed=12 * features * inner, transcendentals=slots * inner
         ),
     )(routes.T, gate_weights.T, tokens, cotangent, weight_gate[0], weight_up[0], weight_down[0])
-    smem = pl.BlockSpec(memory_space=pltpu.SMEM)
     mixed, grad_tokens, grad_gates, grad_gate, grad_up, grad_down = pl.pallas_call(
         finish_kernel,
         out_shape=(
@@ -479,21 +495,18 @@
             gates_shape,
             *weight_shapes,
         ),
-        in_specs=[smem, hbm, vmem, vmem, hbm, hbm, hbm],
+        in_specs=[vmem, vmem, vmem, hbm, hbm, hbm],
         out_specs=(vmem, vmem, vmem, hbm, hbm, hbm),
         scratch_shapes=[
-            pltpu.VMEM((slots, tiles, LANES), bf16),
-            pltpu.VMEM((GROUP, tiles, LANES), bf16),
             pltpu.VMEM((features, inner), bf16),
             pltpu.VMEM((features, inner), bf16),
             pltpu.VMEM((inner, features), bf16),
-            semaphore,
             semaphore((3, PIECES)),
             semaphore((3, PIECES)),
         ],
         compiler_params=pltpu.CompilerParams(vmem_limit_bytes=VMEM_LIMIT),
         cost_estimate=pl.CostEstimate(flops=slots * features, bytes_accessed=12 * features * inner, transcendentals=0),
-    )(slot, d_back, mixed, grad_gates, grad_gate, grad_up, grad_down)
+    )(mixed, grad_tokens, grad_gates, grad_gate, grad_up, grad_down)
     return (mixed, grad_tokens, grad_gates.T, grad_gate[None], grad_up[None], grad_down[None])
 
 

time: 282 us -> 276 us (0.979)
  the two profiles are of different devices: /device:TPU:57 before, /device:TPU:7 now
where the time goes in v5:
time: 276 us
  Pallas kernels  275 us (100%)
    pallas_call x1, Pallas kernels, body(): pl.pallas_call(layer_kernel, out_shape=(jax.ShapeDtypeStruct((count, tile...  266 us
    pallas_call x1, Pallas kernels, body(): pl.pallas_call(finish_kernel, out_shape=(jax.ShapeDtypeStruct(tokens.shap...  9.46 us

profile of v5, /device:TPU:7, one launch (start us, length us, event | category | flops | bytes accessed | tf_op | source)
XLA Modules:
  0.0 275.8 jit_solution(5731401737541537463)
XLA Ops:
  0.6 265.6 %shard_map.118 = (bf16[128,16,128]{2,1,0:T(8,128)(2,1)}, bf16[128,2048]{1,0:T(8,128)(2,1)}, f32[8,128]{1,0:T(8,128)}, bf16[2048,768]{1,0:T(8,128)(2,1)}, bf16[20...) custom-call(s32[8,128]{1,0:T(8,128)} %bitcast.15, f32[8,128]{1,0:T(8,128)} %bitcast.16, ...), custom_call_target="tpu_custom_call" | custom-call | flops 36238786560 | bytes 18874368 | tf_op jit(solution)/shard_map/pallas_call | solution.py:432
  266.3 9.5 %shard_map.119 = (bf16[128,2048]{1,0:T(8,128)(2,1)}, bf16[128,2048]{1,0:T(8,128)(2,1)}, f32[8,128]{1,0:T(8,128)}, bf16[2048,768]{1,0:T(8,128)(2,1)}, bf16[2048,7...) custom-call(bf16[128,16,128]{2,1,0:T(8,128)(2,1)} %get-tuple-element.18.mixed_rows, ...), custom_call_target="tpu_custom_call" | custom-call | flops 2621440 | bytes 18874368 | tf_op jit(solution)/shard_map/pallas_call | solution.py:490

commit v6 on v5

--- a/solution.py
+++ b/solution.py
@@ -385,7 +385,7 @@
 
 def finish_kernel(
     mixed_rows, token_sums, gates, g_gate, g_up, g_down, mixed, grad_tokens, grad_gates, out_gate, out_up, out_down,
-    hold_gate, hold_up, hold_down, in_sem, out_sem,
+    hold_gate, hold_up, hold_down, hold_sums, hold_rows, hold_mixed, in_sem, out_sem,
 ):
     loads, stores = [], []
     for i, (src, held, dst) in enumerate(
@@ -396,20 +396,27 @@
             at = pl.ds(q * part, part)
             loads.append(pltpu.make_async_copy(src.at[at], held.at[at], in_sem.at[i, q]))
             stores.append(pltpu.make_async_copy(held.at[at], dst.at[at], out_sem.at[i, q]))
-    for copy in loads:
+    rows_in = pltpu.make_async_copy(mixed_rows, hold_rows, in_sem.at[3, 0])
+    sums_in = pltpu.make_async_copy(token_sums, hold_sums, in_sem.at[3, 1])
+    mixed_out = pltpu.make_async_copy(hold_mixed, mixed, out_sem.at[3, 0])
+    sums_out = pltpu.make_async_copy(hold_sums, grad_tokens, out_sem.at[3, 1])
+    for copy in (rows_in, sums_in, *loads):
         copy.start()
+    grad_gates[...] = gates[...]
+    rows_in.wait()
+
+    def spread(i):
+        start = pl.multiple_of(i * GROUP, GROUP)
+        rows_to_native(hold_rows[pl.ds(start, GROUP)], hold_mixed, start)
+
+    loop(hold_mixed.shape[0] // GROUP, spread)
+    mixed_out.start()
+    sums_in.wait()
+    sums_out.start()
     for load, store in zip(loads, stores):
         load.wait()
         store.start()
-    grad_gates[...] = gates[...]
-    grad_tokens[...] = token_sums[...]
-
-    def spread(i):
-        start = pl.multiple_of(i * GROUP, GROUP)
-        rows_to_native(mixed_rows[pl.ds(start, GROUP)], mixed, start)
-
-    loop(mixed.shape[0] // GROUP, spread)
-    for copy in stores:
+    for copy in (mixed_out, sums_out, *stores):
         copy.wait()
 
 
@@ -495,14 +502,17 @@
             gates_shape,
             *weight_shapes,
         ),
-        in_specs=[vmem, vmem, vmem, hbm, hbm, hbm],
-        out_specs=(vmem, vmem, vmem, hbm, hbm, hbm),
+        in_specs=[hbm, hbm, vmem, hbm, hbm, hbm],
+        out_specs=(hbm, hbm, vmem, hbm, hbm, hbm),
         scratch_shapes=[
             pltpu.VMEM((features, inner), bf16),
             pltpu.VMEM((features, inner), bf16),
             pltpu.VMEM((inner, features), bf16),
-            semaphore((3, PIECES)),
-            semaphore((3, PIECES)),
+            pltpu.VMEM(tokens.shape, bf16),
+            pltpu.VMEM((count, tiles, LANES), bf16),
+            pltpu.VMEM(tokens.shape, bf16),
+            semaphore((4, PIECES)),
+            semaphore((4, PIECES)),
         ],
         compiler_params=pltpu.CompilerParams(vmem_limit_bytes=VMEM_LIMIT),
         cost_estimate=pl.CostEstimate(flops=slots * features, bytes_accessed=12 * features * inner, transcendentals=0),

time: 276 us -> 276 us (level)
  no operation moved by 1% of the time
where the time goes in v6:
time: 276 us
  Pallas kernels  275 us (100%)
    pallas_call x1, Pallas kernels, body(): pl.pallas_call(layer_kernel, out_shape=(jax.ShapeDtypeStruct((count, tile...  266 us
    pallas_call x1, Pallas kernels, body(): pl.pallas_call(finish_kernel, out_shape=(jax.ShapeDtypeStruct(tokens.shap...  9.25 us

profile of v6, /device:TPU:7, one launch (start us, length us, event | category | flops | bytes accessed | tf_op | source)
XLA Modules:
  0.0 275.5 jit_solution(13669332141236487693)
XLA Ops:
  0.6 265.6 %shard_map.118 = (bf16[128,16,128]{2,1,0:T(8,128)(2,1)}, bf16[128,2048]{1,0:T(8,128)(2,1)}, f32[8,128]{1,0:T(8,128)}, bf16[2048,768]{1,0:T(8,128)(2,1)}, bf16[20...) custom-call(s32[8,128]{1,0:T(8,128)} %bitcast.15, f32[8,128]{1,0:T(8,128)} %bitcast.16, ...), custom_call_target="tpu_custom_call" | custom-call | flops 36238786560 | bytes 18874368 | tf_op jit(solution)/shard_map/pallas_call | solution.py:439
  266.3 9.2 %shard_map.119 = (bf16[128,2048]{1,0:T(8,128)(2,1)}, bf16[128,2048]{1,0:T(8,128)(2,1)}, f32[8,128]{1,0:T(8,128)}, bf16[2048,768]{1,0:T(8,128)(2,1)}, bf16[2048,7...) custom-call(bf16[128,16,128]{2,1,0:T(8,128)(2,1)} %get-tuple-element.18.mixed_rows, ...), custom_call_target="tpu_custom_call" | custom-call | flops 2621440 | bytes 18874368 | tf_op jit(solution)/shard_map/pallas_call | solution.py:497
